TPU v7x, 256 devices: a whole 4x4x8 slice. The times are simulated.
256 devices in a mesh: dp: 32 (over x, z), tensor: 8 (over y, core).
Axes of the slice: x: 4, y: 4, z: 8, core: 2. Of those that a mesh axis runs over, the one named last changes fastest.
Arguments:
- momentum: float32 [32, 128, 28672], P('dp', None, 'tensor'), may hold values from -120 to 120, as said below
- grad: bfloat16 [32, 128, 28672], P('dp', None, 'tensor'), may hold values from -80 to 80, as said below
Outputs:
- new_momentum: float32 [32, 128, 28672], P('dp', None, 'tensor')
- update: float32 [128, 28672], P(None, 'tensor')
Inputs may be any that keep to these rules, and one draw needn't show every extreme that they name: `momentum`: scaled entries. `grad`: scaled entries.
All inputs are finite; a program needn't handle non-finite values.
Results may differ from a plain program's by a relative error of at most 0.0003.
Values sent between devices are 32-bit elements; how exact they have to be, the bound alone decides.
No kernel may reach another device: no remote copies, remote signals or barrier semaphores. Data moves between devices by JAX's collectives and lax.ppermute only.
A program may use at most 64 MiB of HBM per device.

v0:
```python
import math

import jax
import jax.numpy as jnp
from jax import lax
from jax.sharding import PartitionSpec as P

FF = 28672


def dct_lowband():
    samples = jnp.arange(32, dtype=jnp.float32)
    freqs = jnp.arange(8, dtype=jnp.float32)
    weights = jnp.where(freqs == 0.0, math.sqrt(1.0 / 32.0), math.sqrt(2.0 / 32.0))
    return weights[:, None] * jnp.cos(
        math.pi * (2.0 * samples[None, :] + 1.0) * freqs[:, None] / 64.0
    )


def column_matrix():
    inputs = jnp.arange(128, dtype=jnp.int32)[:, None]
    outputs = jnp.arange(32, dtype=jnp.int32)[None, :]
    samples = (inputs % 32).astype(jnp.float32)
    freqs = (outputs % 8).astype(jnp.float32)
    weights = jnp.where(freqs == 0.0, math.sqrt(1.0 / 32.0), math.sqrt(2.0 / 32.0))
    values = weights * jnp.cos(math.pi * (2.0 * samples + 1.0) * freqs / 64.0)
    return jnp.where(inputs // 32 == outputs // 8, values, 0.0)


def local(momentum, grad):
    lowband = dct_lowband()
    across = column_matrix()
    moment = 0.999 * momentum[0] + grad[0].astype(jnp.float32)
    row_count, col_count = moment.shape
    groups = col_count // 128
    row_tiles = row_count // 32
    col_tiles = col_count // 32
    highest = lax.Precision.HIGHEST
    mixed = jnp.dot(moment.reshape(row_count, groups, 128), across, precision=highest)
    mixed = mixed.reshape(row_tiles, 32, col_tiles * 8)
    bands = jnp.einsum("kn,anc->akc", lowband, mixed, precision=highest)
    spread = jnp.einsum("kn,akc->anc", lowband, bands, precision=highest)
    spread = spread.reshape(row_count, groups, 32)
    new_momentum = (
        moment - jnp.dot(spread, across.T, precision=highest).reshape(row_count, col_count)
    )[None]
    flat_bands = bands.reshape(row_tiles, 8, col_tiles, 8).transpose(0, 2, 1, 3).reshape(-1)
    own_bands = lax.psum_scatter(flat_bands, "dp", scatter_dimension=0, tiled=True)
    energy = lax.psum(jnp.sum(own_bands * own_bands), ("dp", "tensor"))
    divisor = jnp.sqrt(energy / (row_count * FF) + 1e-06)
    blocks = own_bands.reshape(-1, 8, 8)
    tile_values = (
        jnp.einsum("kn,tkl,lm->tnm", lowband, blocks, lowband, precision=highest) / divisor
    )
    gathered = lax.all_gather(tile_values.reshape(-1), "dp", axis=0, tiled=True)
    update = (
        gathered.reshape(row_tiles, col_tiles, 32, 32)
        .transpose(0, 2, 1, 3)
        .reshape(row_count, col_count)
    )
    return (new_momentum, update)


def solution(mesh):
    return jax.shard_map(
        local,
        mesh=mesh,
        in_specs=(P("dp", None, "tensor"), P("dp", None, "tensor")),
        out_specs=(P("dp", None, "tensor"), P(None, "tensor")),
        check_vma=False,
    )
```

profile of v0, /device:TPU:1, one launch (start us, length us, event | category | flops | bytes accessed | tf_op | source)
XLA Modules:
  0.0 348.8 jit_solution(11493830788522218994)
XLA Ops:
  7.3 1.7 copy.17
  9.0 1.7 copy.16
  10.7 1.7 convert_add_fusion
  12.3 1.2 fusion.7
  13.5 2.0 reshape.172
  15.6 3.2 fusion.2
  18.8 2.2 reshape.175
  21.0 3.3 copy.21
  24.3 2.9 reshape.176
  27.3 0.6 dynamic-slice
  28.6 138.8 %all-reduce.3.cloned.1.call-done = f32[28672]{0:T(1024)} async-done(((f32[28672]{0:T(1024)}), f32[28672]{0:T(1024)}) %all-reduce.3.cloned.1.call-update) | async-done | bytes 114704
  167.3 1.4 multiply_reduce_fusion
  168.7 78.6 %psum.7 = f32[]{:T(128)} all-reduce(f32[]{:T(128)} %get-tuple-element.6), channel_id=1, replica_groups=mesh['dp'=32,'tensor'=8] {'dp','tensor'}, use_global_device_ids=true, to_apply=%region_2.3 | all-reduce | flops 1 | bytes 8 | tf_op jit(solution)/shard_map/psum | solution.py:49
  249.0 0.7 reshape.178
  249.7 0.6 convolution_bitcast_fusion
  250.4 1.7 copy.20
  252.0 2.3 reshape.173
  254.4 1.8 fusion.5
  256.1 1.5 bitcast_subtract_fusion
  257.6 2.7 copy.24
  260.3 59.3 %all-gather.2.cloned.1.call-done = f32[458752]{0:T(1024)} async-done(((f32[14336]{0:T(1024)}), f32[458752]{0:T(1024)}) %all-gather.2.cloned.1.call-update) | async-done | bytes 1835024 | tf_op jit(solution)/shard_map/all_gather | solution.py:55
  319.7 5.6 %reshape.179 = f32[4,112,32,32]{3,2,1,0:T(8,128)} reshape(f32[458752]{0:T(1024)} %all-gather.2.cloned.1.call-done) | data formatting | bytes 3670016 | tf_op jit(solution)/shard_map/reshape | solution.py:57
  325.2 10.3 %copy.23 = f32[4,32,112,32]{3,2,1,0:T(8,128)} copy(f32[4,32,112,32]{3,1,2,0:T(8,128)} %bitcast.37) | data formatting | bytes 3670016 | tf_op jit(solution)/shard_map/transpose | solution.py:58
  335.6 6.4 %reshape.180 = f32[128,3584]{1,0:T(8,128)} reshape(f32[4,32,112,32]{3,2,1,0:T(8,128)} %copy.23) | data formatting | bytes 3670016 | tf_op jit(solution)/shard_map/reshape | solution.py:59
  (17 shorter events, 1.1 us)
Async XLA Ops:
  7.2 1.8 copy-start
  7.2 160.2 %all-reduce.3.cloned.1.call-start = ((), (), s32[]{:S(2)}) async-start(), calls=%async_computation.1 | async-start | bytes 229376
  24.3 3.0 copy-start.1
  27.3 292.4 %all-gather.2.cloned.1.call-start = ((), (), s32[]{:S(2)}) async-start(), calls=%async_computation | async-start | bytes 1892352 | tf_op jit(solution)/shard_map/all_gather | solution.py:55
Sparse Core Ops, SparseCore 0:
  27.4 139.8 all-reduce.2
  249.8 69.7 all-gather.1
where the time goes:
time: 352 us; the launch traced here: 349 us
  waiting for transfers between devices  198 us (56%)
  blocking collectives  78.6 us (22%)
  local copies, waits for them, and re-layouts  44.2 us (13%)
  between operations  15.5 us (4%)
  matrix products  7.65 us (2%)
  other arithmetic  4.56 us (1%)
    unnamed x3, waiting for transfers between devices  139 us
    psum x1, blocking collectives, local(): energy = lax.psum(jnp.sum(own_bands * own_bands), ('dp', 'tensor'))  78.6 us
    all_gather x1, waiting for transfers between devices, local(): gathered = lax.all_gather(tile_values.reshape(-1), 'dp', axis=0, tiled=True)  59.3 us
    transpose x1, local copies, waits for them, and re-layouts, local(): update = gathered.reshape(row_tiles, col_tiles, 32, 32).transpose(0, 2, 1...  10.3 us
  transfers between devices with their start and end apart: 2, of which 2 were waited for; matrix products, arithmetic and copies ran while one was open for 3% of the time, Pallas kernels for 0%

commit v1 on v0

v1 whole, which is shorter than its diff:
```python
import math

import jax
import jax.numpy as jnp
import ml_dtypes
import numpy as np
from jax import lax
from jax.experimental import pallas as pl
from jax.experimental.pallas import tpu as pltpu
from jax.sharding import PartitionSpec as P

FF = 28672
ROWS = 128
CHUNK = 512
F32 = jnp.float32
BF16 = jnp.bfloat16
HBM = pl.BlockSpec(memory_space=pltpu.HBM)
VMEM = pl.BlockSpec(memory_space=pltpu.VMEM)


def lowband():
    samples = np.arange(32, dtype=np.float64)
    freqs = np.arange(8, dtype=np.float64)
    weights = np.where(freqs == 0.0, math.sqrt(1.0 / 32.0), math.sqrt(2.0 / 32.0))
    return weights[:, None] * np.cos(math.pi * (2.0 * samples[None] + 1.0) * freqs[:, None] / 64.0)


def split(values):
    high = values.astype(ml_dtypes.bfloat16)
    low = (values - high.astype(np.float64)).astype(ml_dtypes.bfloat16)
    return high, low


def tables():
    low = lowband()
    row_high, row_low = split(np.kron(np.eye(ROWS // 32), low))
    col_high, col_low = split(np.kron(np.eye(CHUNK // 32), low.T))
    zero = np.zeros_like(row_high)
    row_enc = np.block([[row_high, row_high], [row_low, zero]])
    col_enc = np.concatenate([col_high, col_low], axis=1)
    row_dec = np.concatenate([row_high.T, row_high.T, row_low.T], axis=1)
    pad = np.zeros((ROWS, 32), ml_dtypes.bfloat16)
    row_dec = np.concatenate([row_dec, pad], axis=1)
    col_dec = np.concatenate([col_high.T, col_high.T, col_low.T], axis=0)
    return row_enc, col_enc, row_dec, col_dec


def dot(a, b):
    return jnp.dot(a, b, preferred_element_type=F32)


def halves(x):
    high = x.astype(BF16)
    return high, (x - high.astype(F32)).astype(BF16)


def encode_kernel(chunks, m_hbm, g_hbm, row_hbm, col_hbm, bands_ref, m, g, row, col, mixed, sems):
    copies = []
    for i in range(chunks):
        cols = pl.ds(i * CHUNK, CHUNK)
        copies.append(
            (
                pltpu.make_async_copy(m_hbm.at[:, cols], m.at[i], sems.at[0, i]),
                pltpu.make_async_copy(g_hbm.at[:, cols], g.at[i], sems.at[1, i]),
            )
        )
    tables_in = (
        pltpu.make_async_copy(row_hbm, row, sems.at[0, chunks]),
        pltpu.make_async_copy(col_hbm, col, sems.at[1, chunks]),
    )
    tables_in[0].start()
    for pair in copies:
        pair[0].start()
        pair[1].start()
    tables_in[1].start()
    tables_in[0].wait()
    for i in range(chunks):
        copies[i][0].wait()
        copies[i][1].wait()
        moment = 0.999 * m[i] + g[i].astype(F32)
        both = dot(row[...], jnp.concatenate(halves(moment), axis=0))
        mixed[pl.ds(i * 32, 32), :] = both[:32] + both[32:]
    tables_in[1].wait()
    high, low = halves(mixed[...])
    first = dot(high, col[...])
    bands_ref[...] = first[:, :128] + first[:, 128:] + dot(low, col[:, :128])


def expand(bands, row, col):
    high, low = halves(bands)
    return dot(jnp.concatenate([high, low, high], axis=1), col)


def rows_of(part, row):
    high, low = halves(part)
    stack = jnp.concatenate([high, low, high, jnp.zeros_like(high)], axis=0)
    return dot(row, stack)


def residual_kernel(chunks, m_hbm, g_hbm, bands_ref, row_ref, col_ref, out_hbm, m, g, spread, sems):
    loads, stores = [], []
    for i in range(chunks):
        cols = pl.ds(i * CHUNK, CHUNK)
        loads.append(
            (
                pltpu.make_async_copy(m_hbm.at[:, cols], m.at[i], sems.at[0, i]),
                pltpu.make_async_copy(g_hbm.at[:, cols], g.at[i], sems.at[1, i]),
            )
        )
        stores.append(pltpu.make_async_copy(m.at[i], out_hbm.at[:, cols], sems.at[2, i]))
    for pair in loads:
        pair[0].start()
        pair[1].start()
    spread[...] = expand(bands_ref[...], row_ref[...], col_ref[...])
    for i in range(chunks):
        loads[i][0].wait()
        loads[i][1].wait()
        moment = 0.999 * m[i] + g[i].astype(F32)
        m[i] = moment - rows_of(spread[pl.ds(i * 32, 32), :], row_ref[...])
        stores[i].start()
    for store in stores:
        store.wait()


def update_kernel(chunks, bands_ref, energy_ref, row_ref, col_ref, out_hbm, out, spread, sems):
    energy = jnp.sum(energy_ref[...])
    scale = lax.rsqrt(jnp.full((1, 128), energy * (1.0 / (ROWS * FF)) + 1e-06, F32))
    spread[...] = expand(bands_ref[...] * scale, row_ref[...], col_ref[...])
    stores = []
    for i in range(chunks):
        cols = pl.ds(i * CHUNK, CHUNK)
        out[i] = rows_of(spread[pl.ds(i * 32, 32), :], row_ref[...])
        stores.append(pltpu.make_async_copy(out.at[i], out_hbm.at[:, cols], sems.at[i]))
        stores[-1].start()
    for store in stores:
        store.wait()


PARAMS = pltpu.CompilerParams(vmem_limit_bytes=24 * 1024 * 1024)


def in_hbm(x):
    return pltpu.with_memory_space_constraint(x, pltpu.HBM)


def encode(m, g, row, col):
    chunks = m.shape[1] // CHUNK
    return pl.pallas_call(
        lambda *refs: encode_kernel(chunks, *refs),
        out_shape=jax.ShapeDtypeStruct((chunks * 32, 128), F32),
        in_specs=[HBM] * 4,
        out_specs=VMEM,
        scratch_shapes=[
            pltpu.VMEM((chunks, ROWS, CHUNK), F32),
            pltpu.VMEM((chunks, ROWS, CHUNK), BF16),
            pltpu.VMEM(row.shape, BF16),
            pltpu.VMEM(col.shape, BF16),
            pltpu.VMEM((chunks * 32, CHUNK), F32),
            pltpu.SemaphoreType.DMA((2, chunks + 1)),
        ],
        compiler_params=PARAMS,
        cost_estimate=pl.CostEstimate(flops=4 * 10**7, bytes_accessed=3 * 10**6, transcendentals=0),
        name="encode",
    )(*(in_hbm(a) for a in (m, g, row, col)))


def residual(m, g, bands, row, col):
    chunks = m.shape[1] // CHUNK
    return pl.pallas_call(
        lambda *refs: residual_kernel(chunks, *refs),
        out_shape=jax.ShapeDtypeStruct(m.shape, F32),
        in_specs=[HBM, HBM, VMEM, VMEM, VMEM],
        out_specs=HBM,
        scratch_shapes=[
            pltpu.VMEM((chunks, ROWS, CHUNK), F32),
            pltpu.VMEM((chunks, ROWS, CHUNK), BF16),
            pltpu.VMEM((chunks * 32, CHUNK), F32),
            pltpu.SemaphoreType.DMA((3, chunks)),
        ],
        compiler_params=PARAMS,
        cost_estimate=pl.CostEstimate(flops=4 * 10**7, bytes_accessed=5 * 10**6, transcendentals=0),
        name="residual",
    )(in_hbm(m), in_hbm(g), bands, row, col)


def decode(bands, energy, row, col):
    chunks = bands.shape[0] // 32
    return pl.pallas_call(
        lambda *refs: update_kernel(chunks, *refs),
        out_shape=jax.ShapeDtypeStruct((ROWS, chunks * CHUNK), F32),
        in_specs=[VMEM] * 4,
        out_specs=HBM,
        scratch_shapes=[
            pltpu.VMEM((chunks, ROWS, CHUNK), F32),
            pltpu.VMEM((chunks * 32, CHUNK), F32),
            pltpu.SemaphoreType.DMA((chunks,)),
        ],
        compiler_params=PARAMS,
        cost_estimate=pl.CostEstimate(flops=4 * 10**7, bytes_accessed=2 * 10**6, transcendentals=0),
        name="decode",
    )(bands, energy, row, col)


def partners(pairs):
    other = {}
    for a, b in pairs:
        other[a], other[b] = b, a
    return other


def along_z(pairs):
    other = partners(pairs)
    return [(8 * x + z, 8 * x + other[z]) for x in range(4) for z in range(8)]


def along_x(pairs):
    other = partners(pairs)
    return [(8 * x + z, 8 * other[x] + z) for x in range(4) for z in range(8)]


EXCHANGES = (
    along_z([(0, 1), (2, 3), (4, 5), (6, 7)]),
    along_z([(1, 2), (3, 4), (5, 6), (7, 0)]),
    along_z([(0, 3), (1, 6), (2, 5), (4, 7)]),
    along_x([(0, 1), (2, 3)]),
    along_x([(1, 2), (3, 0)]),
)


def local(momentum, grad):
    row_enc, col_enc, row_dec, col_dec = (jnp.asarray(t) for t in tables())
    momentum, grad = momentum[0], grad[0]
    bands = encode(momentum, grad, row_enc, col_enc)
    new_momentum = residual(momentum, grad, bands, row_dec, col_dec)
    summed = bands
    for step, pairs in enumerate(EXCHANGES):
        summed = summed + lax.ppermute(summed, "dp", pairs)
        if step == 2:
            summed, new_momentum = lax.optimization_barrier((summed, new_momentum))
    squares = jnp.sum((summed * summed).reshape(-1, 8, 128), axis=0)
    energy = lax.all_to_all(jnp.broadcast_to(squares[None], (8, 8, 128)), "tensor", 0, 0)
    update = decode(summed, energy.reshape(64, 128), row_dec, col_dec)
    return (new_momentum[None], update)


def solution(mesh):
    return jax.shard_map(
        local,
        mesh=mesh,
        in_specs=(P("dp", None, "tensor"), P("dp", None, "tensor")),
        out_specs=(P("dp", None, "tensor"), P(None, "tensor")),
        check_vma=False,
    )
```

time: 352 us -> 48.2 us (0.14)
  waiting for transfers between devices: 198 us -> 11.1 us
  blocking collectives: 78.6 us -> 14.4 us
  local copies, waits for them, and re-layouts: 44.2 us -> 0.02 us
  between operations: 15.5 us -> 0.68 us
  starting transfers between devices: 0.08 us -> 14 us
  Pallas kernels: 0 us -> 7.78 us
  matrix products: 7.65 us -> 0 us
  other arithmetic: 4.56 us -> 0.09 us
    unnamed x3 -> x0, waiting for transfers between devices: 139 us -> none
    psum x1 -> x0, blocking collectives: 78.6 us -> none  [local(): energy = lax.psum(jnp.sum(own_bands * own_bands), ('dp', 'tensor'))]
    all_gather x1 -> x0, waiting for transfers between devices: 59.3 us -> none  [local(): gathered = lax.all_gather(tile_values.reshape(-1), 'dp', axis=0, tiled=True)]
    reshape x8 -> x0, local copies, waits for them, and re-layouts: 22.2 us -> none  [the longest x1 6.35 us: local(): update = gathered.reshape(row_tiles, col_tiles, 32, 32).transpose(0, 2, 1...]
    transpose x3 -> x0, local copies, waits for them, and re-layouts: 15.3 us -> none  [the longest x1 10.3 us: local(): update = gathered.reshape(row_tiles, col_tiles, 32, 32).transpose(0, 2, 1...]
    all_to_all x0 -> x1, blocking collectives: none -> 14.4 us  [local(): lax.all_to_all(jnp.broadcast_to(squares[None], (8, 8, 128)), 'tensor', 0, 0)]
    ppermute x0 -> x5, starting transfers between devices: none -> 14 us  [local(): summed = summed + lax.ppermute(summed, 'dp', pairs)]
    ppermute x0 -> x5, waiting for transfers between devices: none -> 11.1 us  [local(): summed = summed + lax.ppermute(summed, 'dp', pairs)]
  transfers between devices with their start and end apart: 2 -> 5, of which waited for: 2 -> 5; matrix products, arithmetic and copies ran while one was open for 3% -> 0% of each run, Pallas kernels for 0% -> 7%
where the time goes in v1:
time: 48.2 us; the launch traced here: 48 us
  blocking collectives  14.4 us (30%)
  starting transfers between devices  14 us (29%)
  waiting for transfers between devices  11.1 us (23%)
  Pallas kernels  7.78 us (16%)
  between operations  0.68 us (1%)
    all_to_all x1, blocking collectives, local(): lax.all_to_all(jnp.broadcast_to(squares[None], (8, 8, 128)), 'tensor', 0, 0)  14.4 us
    ppermute x5, starting transfers between devices, local(): summed = summed + lax.ppermute(summed, 'dp', pairs)  14 us
    ppermute x5, waiting for transfers between devices, local(): summed = summed + lax.ppermute(summed, 'dp', pairs)  11.1 us
    pallas_call x1, Pallas kernels, residual(): pl.pallas_call(lambda *refs: residual_kernel(chunks, *refs), out_shape=ja...  3.15 us
    pallas_call x1, Pallas kernels, encode(): pl.pallas_call(lambda *refs: encode_kernel(chunks, *refs), out_shape=jax....  2.85 us
    pallas_call x1, Pallas kernels, decode(): pl.pallas_call(lambda *refs: update_kernel(chunks, *refs), out_shape=jax....  1.79 us
  transfers between devices with their start and end apart: 5, of which 5 were waited for; matrix products, arithmetic and copies ran while one was open for 0% of the time, Pallas kernels for 7%

profile of v1, /device:TPU:1, one launch (start us, length us, event | category | flops | bytes accessed | tf_op | source)
XLA Modules:
  0.0 48.0 jit_solution(9248898477826239127)
XLA Ops:
  0.6 0.0 copy-start
  0.6 0.0 copy-start.1
  0.7 2.9 %encode.1.refs_2_ = f32[224,128]{1,0:T(8,128)S(1)} custom-call(f32[128,3584]{1,0:T(8,128)} %bitcast.7, bf16[128,3584]{1,0:T(8,128)(2,1)} %bitcast.9, bf16[64,256]{1,0:T(8,128)(2,1)} %constant.10.clone.refs_2_, bf16[512,256]{1,0:T(8,128)(2,1)} %constant.11.clone.refs_3_), custom_call_target="tpu_custom_call" | custom-call | flops 40000000 | bytes 3000000 | tf_op jit(solution)/shard_map/encode/pallas_call | solution.py:148
  3.5 2.6 %collective-permute-start = (f32[224,128]{1,0:T(8,128)S(1)}, f32[224,128]{1,0:T(8,128)S(1)}, u32[]{:S(2)}, u32[]{:S(2)}) collective-permute-start(f32[224,128]{1,0:T(8,128)S(1)} %encode.1.refs_2_), channel_id=1, source_target_pairs={{0,8},{8,0},{16,24},{24,16},{32,40},{40,32},{48,56},{56,48},{64,72... | collective-permute-start | bytes 344072 | tf_op jit(solution)/shard_map/ppermute | solution.py:237
  6.1 2.2 %collective-permute-done = f32[224,128]{1,0:T(8,128)S(1)} collective-permute-done((f32[224,128]{1,0:T(8,128)S(1)}, f32[224,128]{1,0:T(8,128)S(1)}, u32[]{:S(2)}, u32[]{:S(2)}) %collective-permute-start) | collective-permute-done | bytes 114720 | tf_op jit(solution)/shard_map/ppermute | solution.py:237
  8.3 5.9 %collective-permute-start.1 = (f32[224,128]{1,0:T(8,128)S(1)}, f32[224,128]{1,0:T(8,128)S(1)}, u32[]{:S(2)}, u32[]{:S(2)}) collective-permute-start(f32[224,128]{1,0:T(8,128)S(1)} %add.15), channel_id=1, source_target_pairs={{0,56},{8,16},{16,8},{24,32},{32,24},{40,48},{48,40},{56,0},{64,12... | collective-permute-start | bytes 344072 | tf_op jit(solution)/shard_map/ppermute | solution.py:237
  14.1 2.2 %collective-permute-done.1 = f32[224,128]{1,0:T(8,128)S(1)} collective-permute-done((f32[224,128]{1,0:T(8,128)S(1)}, f32[224,128]{1,0:T(8,128)S(1)}, u32[]{:S(2)}, u32[]{:S(2)}) %collective-permute-start.1) | collective-permute-done | bytes 114720 | tf_op jit(solution)/shard_map/ppermute | solution.py:237
  16.3 1.7 %collective-permute-start.2 = (f32[224,128]{1,0:T(8,128)S(1)}, f32[224,128]{1,0:T(8,128)S(1)}, u32[]{:S(2)}, u32[]{:S(2)}) collective-permute-start(f32[224,128]{1,0:T(8,128)S(1)} %add.16), channel_id=1, source_target_pairs={{0,24},{8,48},{16,40},{24,0},{32,56},{40,16},{48,8},{56,32},{64,88... | collective-permute-start | bytes 344072 | tf_op jit(solution)/shard_map/ppermute | solution.py:237
  18.0 0.0 copy-done
  18.0 0.0 copy-done.1
  18.0 3.1 %residual.1 = f32[128,3584]{1,0:T(8,128)} custom-call(f32[128,3584]{1,0:T(8,128)} %bitcast.8, bf16[128,3584]{1,0:T(8,128)(2,1)} %bitcast.10, f32[224,128]{1,0:T(8,128)S(1)} %encode.1.refs_2_, bf16[128,128]{1,0:T(8,128)(2,1)S(1)} %copy-done.1, bf16[384,512]{1,0:T(8,128)(2,1)S(1)} %copy-done), custom_call_target="tpu_custom_call" | custom-call | flops 40000000 | bytes 5000000 | tf_op jit(solution)/shard_map/residual/pallas_call | solution.py:169
  21.2 1.9 %collective-permute-done.2 = f32[224,128]{1,0:T(8,128)S(1)} collective-permute-done((f32[224,128]{1,0:T(8,128)S(1)}, f32[224,128]{1,0:T(8,128)S(1)}, u32[]{:S(2)}, u32[]{:S(2)}) %collective-permute-start.2) | collective-permute-done | bytes 114720 | tf_op jit(solution)/shard_map/ppermute | solution.py:237
  23.1 1.3 %collective-permute-start.3 = (f32[224,128]{1,0:T(8,128)S(1)}, f32[224,128]{1,0:T(8,128)S(1)}, u32[]{:S(2)}, u32[]{:S(2)}) collective-permute-start(f32[224,128]{1,0:T(8,128)S(1)} %add.17), channel_id=1, source_target_pairs={{0,64},{8,72},{16,80},{24,88},{32,96},{40,104},{48,112},{56,120},{... | collective-permute-start | bytes 344072 | tf_op jit(solution)/shard_map/ppermute | solution.py:237
  24.4 2.4 %collective-permute-done.3 = f32[224,128]{1,0:T(8,128)S(1)} collective-permute-done((f32[224,128]{1,0:T(8,128)S(1)}, f32[224,128]{1,0:T(8,128)S(1)}, u32[]{:S(2)}, u32[]{:S(2)}) %collective-permute-start.3) | collective-permute-done | bytes 114720 | tf_op jit(solution)/shard_map/ppermute | solution.py:237
  26.9 2.6 %collective-permute-start.4 = (f32[224,128]{1,0:T(8,128)S(1)}, f32[224,128]{1,0:T(8,128)S(1)}, u32[]{:S(2)}, u32[]{:S(2)}) collective-permute-start(f32[224,128]{1,0:T(8,128)S(1)} %add.18), channel_id=1, source_target_pairs={{0,192},{8,200},{16,208},{24,216},{32,224},{40,232},{48,240},{56,2... | collective-permute-start | bytes 344072 | tf_op jit(solution)/shard_map/ppermute | solution.py:237
  29.4 2.4 %collective-permute-done.4 = f32[224,128]{1,0:T(8,128)S(1)} collective-permute-done((f32[224,128]{1,0:T(8,128)S(1)}, f32[224,128]{1,0:T(8,128)S(1)}, u32[]{:S(2)}, u32[]{:S(2)}) %collective-permute-start.4) | collective-permute-done | bytes 114720 | tf_op jit(solution)/shard_map/ppermute | solution.py:237
  31.8 14.4 %all_to_all.5 = f32[8,8,128]{2,1,0:T(8,128)S(1)} all-to-all(f32[8,8,128]{2,1,0:T(8,128)S(1)} %broadcast_in_dim.10), channel_id=1, replica_groups=mesh['dp'=32,'tensor'=8] {'tensor'}, dimensions={0} | all-to-all | bytes 65536 | tf_op jit(solution)/shard_map/all_to_all | solution.py:241
  46.2 1.8 %decode.1 = f32[128,3584]{1,0:T(8,128)} custom-call(f32[224,128]{1,0:T(8,128)S(1)} %get-tuple-element.7.refs_0_, f32[64,128]{1,0:T(8,128)S(1)} %bitcast.6, bf16[128,128]{1,0:T(8,128)(2,1)S(1)} %copy-done.1, bf16[384,512]{1,0:T(8,128)(2,1)S(1)} %copy-done), custom_call_target="tpu_custom_call" | custom-call | flops 40000000 | bytes 2000000 | tf_op jit(solution)/shard_map/decode/pallas_call | solution.py:188
  (6 shorter events, 0.1 us)
Async XLA Ops:
  0.6 17.4 %copy-start = (bf16[384,512]{1,0:T(8,128)(2,1)S(1)}, bf16[384,512]{1,0:T(8,128)(2,1)}, u32[]{:S(2)}) copy-start(bf16[384,512]{1,0:T(8,128)(2,1)} %constant.13.clone.refs_4_.refs_3_) | copy-start | bytes 1179652
  0.6 17.4 %copy-start.1 = (bf16[128,128]{1,0:T(8,128)(2,1)S(1)}, bf16[128,128]{1,0:T(8,128)(2,1)}, u32[]{:S(2)}) copy-start(bf16[128,128]{1,0:T(8,128)(2,1)} %constant.12.clone.refs_3_.refs_2_) | copy-start | bytes 98308
  3.5 4.7 %collective-permute-start = (f32[224,128]{1,0:T(8,128)S(1)}, f32[224,128]{1,0:T(8,128)S(1)}, u32[]{:S(2)}, u32[]{:S(2)}) collective-permute-start(f32[224,128]{1,0:T(8,128)S(1)} %encode.1.refs_2_), channel_id=1, source_target_pairs={{0,8},{8,0},{16,24},{24,16},{32,40},{40,32},{48,56},{56,48},{64,72... | collective-permute-start | bytes 344072 | tf_op jit(solution)/shard_map/ppermute | solution.py:237
  8.3 8.0 %collective-permute-start.1 = (f32[224,128]{1,0:T(8,128)S(1)}, f32[224,128]{1,0:T(8,128)S(1)}, u32[]{:S(2)}, u32[]{:S(2)}) collective-permute-start(f32[224,128]{1,0:T(8,128)S(1)} %add.15), channel_id=1, source_target_pairs={{0,56},{8,16},{16,8},{24,32},{32,24},{40,48},{48,40},{56,0},{64,12... | collective-permute-start | bytes 344072 | tf_op jit(solution)/shard_map/ppermute | solution.py:237
  16.3 6.8 %collective-permute-start.2 = (f32[224,128]{1,0:T(8,128)S(1)}, f32[224,128]{1,0:T(8,128)S(1)}, u32[]{:S(2)}, u32[]{:S(2)}) collective-permute-start(f32[224,128]{1,0:T(8,128)S(1)} %add.16), channel_id=1, source_target_pairs={{0,24},{8,48},{16,40},{24,0},{32,56},{40,16},{48,8},{56,32},{64,88... | collective-permute-start | bytes 344072 | tf_op jit(solution)/shard_map/ppermute | solution.py:237
  23.1 3.7 %collective-permute-start.3 = (f32[224,128]{1,0:T(8,128)S(1)}, f32[224,128]{1,0:T(8,128)S(1)}, u32[]{:S(2)}, u32[]{:S(2)}) collective-permute-start(f32[224,128]{1,0:T(8,128)S(1)} %add.17), channel_id=1, source_target_pairs={{0,64},{8,72},{16,80},{24,88},{32,96},{40,104},{48,112},{56,120},{... | collective-permute-start | bytes 344072 | tf_op jit(solution)/shard_map/ppermute | solution.py:237
  26.9 4.9 %collective-permute-start.4 = (f32[224,128]{1,0:T(8,128)S(1)}, f32[224,128]{1,0:T(8,128)S(1)}, u32[]{:S(2)}, u32[]{:S(2)}) collective-permute-start(f32[224,128]{1,0:T(8,128)S(1)} %add.18), channel_id=1, source_target_pairs={{0,192},{8,200},{16,208},{24,216},{32,224},{40,232},{48,240},{56,2... | collective-permute-start | bytes 344072 | tf_op jit(solution)/shard_map/ppermute | solution.py:237

commit v2 on v1

--- a/solution.py
+++ b/solution.py
@@ -54,7 +54,14 @@
     return high, (x - high.astype(F32)).astype(BF16)
 
 
-def encode_kernel(chunks, m_hbm, g_hbm, row_hbm, col_hbm, bands_ref, m, g, row, col, mixed, sems):
+def ordered(first, second):
+    odd = lax.rem(lax.axis_index("dp") // 8, 2) == 1
+    return jnp.where(odd, second, first), jnp.where(odd, first, second)
+
+
+def encode_kernel(
+    chunks, m_hbm, g_hbm, row_hbm, col_hbm, moment_ref, bands_ref, keep_ref, send_ref, m, g, row, col, mixed, sems
+):
     copies = []
     for i in range(chunks):
         cols = pl.ds(i * CHUNK, CHUNK)
@@ -78,12 +85,16 @@
         copies[i][0].wait()
         copies[i][1].wait()
         moment = 0.999 * m[i] + g[i].astype(F32)
+        moment_ref[i] = moment
         both = dot(row[...], jnp.concatenate(halves(moment), axis=0))
         mixed[pl.ds(i * 32, 32), :] = both[:32] + both[32:]
     tables_in[1].wait()
     high, low = halves(mixed[...])
     first = dot(high, col[...])
-    bands_ref[...] = first[:, :128] + first[:, 128:] + dot(low, col[:, :128])
+    bands = first[:, :128] + first[:, 128:] + dot(low, col[:, :128])
+    bands_ref[...] = bands
+    half = bands.shape[0] // 2
+    keep_ref[...], send_ref[...] = ordered(bands[:half], bands[half:])
 
 
 def expand(bands, row, col):
@@ -97,35 +108,23 @@
     return dot(row, stack)
 
 
-def residual_kernel(chunks, m_hbm, g_hbm, bands_ref, row_ref, col_ref, out_hbm, m, g, spread, sems):
-    loads, stores = [], []
+def residual_kernel(chunks, moment_ref, bands_ref, row_ref, col_ref, out_hbm, out, spread, sems):
+    spread[...] = expand(bands_ref[...], row_ref[...], col_ref[...])
+    stores = []
     for i in range(chunks):
         cols = pl.ds(i * CHUNK, CHUNK)
-        loads.append(
-            (
-                pltpu.make_async_copy(m_hbm.at[:, cols], m.at[i], sems.at[0, i]),
-                pltpu.make_async_copy(g_hbm.at[:, cols], g.at[i], sems.at[1, i]),
-            )
-        )
-        stores.append(pltpu.make_async_copy(m.at[i], out_hbm.at[:, cols], sems.at[2, i]))
-    for pair in loads:
-        pair[0].start()
-        pair[1].start()
-    spread[...] = expand(bands_ref[...], row_ref[...], col_ref[...])
-    for i in range(chunks):
-        loads[i][0].wait()
-        loads[i][1].wait()
-        moment = 0.999 * m[i] + g[i].astype(F32)
-        m[i] = moment - rows_of(spread[pl.ds(i * 32, 32), :], row_ref[...])
-        stores[i].start()
+        out[i] = moment_ref[i] - rows_of(spread[pl.ds(i * 32, 32), :], row_ref[...])
+        stores.append(pltpu.make_async_copy(out.at[i], out_hbm.at[:, cols], sems.at[i]))
+        stores[-1].start()
     for store in stores:
         store.wait()
 
 
-def update_kernel(chunks, bands_ref, energy_ref, row_ref, col_ref, out_hbm, out, spread, sems):
+def update_kernel(chunks, own_ref, other_ref, energy_ref, row_ref, col_ref, out_hbm, out, spread, sems):
     energy = jnp.sum(energy_ref[...])
     scale = lax.rsqrt(jnp.full((1, 128), energy * (1.0 / (ROWS * FF)) + 1e-06, F32))
-    spread[...] = expand(bands_ref[...] * scale, row_ref[...], col_ref[...])
+    bands = jnp.concatenate(ordered(own_ref[...], other_ref[...]), axis=0)
+    spread[...] = expand(bands * scale, row_ref[...], col_ref[...])
     stores = []
     for i in range(chunks):
         cols = pl.ds(i * CHUNK, CHUNK)
@@ -147,9 +146,10 @@
     chunks = m.shape[1] // CHUNK
     return pl.pallas_call(
         lambda *refs: encode_kernel(chunks, *refs),
-        out_shape=jax.ShapeDtypeStruct((chunks * 32, 128), F32),
+        out_shape=[jax.ShapeDtypeStruct((chunks, ROWS, CHUNK), F32)]
+        + [jax.ShapeDtypeStruct((rows, 128), F32) for rows in (chunks * 32, chunks * 16, chunks * 16)],
         in_specs=[HBM] * 4,
-        out_specs=VMEM,
+        out_specs=[VMEM] * 4,
         scratch_shapes=[
             pltpu.VMEM((chunks, ROWS, CHUNK), F32),
             pltpu.VMEM((chunks, ROWS, CHUNK), BF16),
@@ -164,29 +164,10 @@
     )(*(in_hbm(a) for a in (m, g, row, col)))
 
 
-def residual(m, g, bands, row, col):
-    chunks = m.shape[1] // CHUNK
+def residual(moment, bands, row, col):
+    chunks = moment.shape[0]
     return pl.pallas_call(
         lambda *refs: residual_kernel(chunks, *refs),
-        out_shape=jax.ShapeDtypeStruct(m.shape, F32),
-        in_specs=[HBM, HBM, VMEM, VMEM, VMEM],
-        out_specs=HBM,
-        scratch_shapes=[
-            pltpu.VMEM((chunks, ROWS, CHUNK), F32),
-            pltpu.VMEM((chunks, ROWS, CHUNK), BF16),
-            pltpu.VMEM((chunks * 32, CHUNK), F32),
-            pltpu.SemaphoreType.DMA((3, chunks)),
-        ],
-        compiler_params=PARAMS,
-        cost_estimate=pl.CostEstimate(flops=4 * 10**7, bytes_accessed=5 * 10**6, transcendentals=0),
-        name="residual",
-    )(in_hbm(m), in_hbm(g), bands, row, col)
-
-
-def decode(bands, energy, row, col):
-    chunks = bands.shape[0] // 32
-    return pl.pallas_call(
-        lambda *refs: update_kernel(chunks, *refs),
         out_shape=jax.ShapeDtypeStruct((ROWS, chunks * CHUNK), F32),
         in_specs=[VMEM] * 4,
         out_specs=HBM,
@@ -196,9 +177,27 @@
             pltpu.SemaphoreType.DMA((chunks,)),
         ],
         compiler_params=PARAMS,
+        cost_estimate=pl.CostEstimate(flops=4 * 10**7, bytes_accessed=5 * 10**6, transcendentals=0),
+        name="residual",
+    )(moment, bands, row, col)
+
+
+def decode(own, other, energy, row, col):
+    chunks = own.shape[0] // 16
+    return pl.pallas_call(
+        lambda *refs: update_kernel(chunks, *refs),
+        out_shape=jax.ShapeDtypeStruct((ROWS, chunks * CHUNK), F32),
+        in_specs=[VMEM] * 5,
+        out_specs=HBM,
+        scratch_shapes=[
+            pltpu.VMEM((chunks, ROWS, CHUNK), F32),
+            pltpu.VMEM((chunks * 32, CHUNK), F32),
+            pltpu.SemaphoreType.DMA((chunks,)),
+        ],
+        compiler_params=PARAMS,
         cost_estimate=pl.CostEstimate(flops=4 * 10**7, bytes_accessed=2 * 10**6, transcendentals=0),
         name="decode",
-    )(bands, energy, row, col)
+    )(own, other, energy, row, col)
 
 
 def partners(pairs):
@@ -218,28 +217,39 @@
     return [(8 * x + z, 8 * other[x] + z) for x in range(4) for z in range(8)]
 
 
-EXCHANGES = (
-    along_z([(0, 1), (2, 3), (4, 5), (6, 7)]),
-    along_z([(1, 2), (3, 4), (5, 6), (7, 0)]),
-    along_z([(0, 3), (1, 6), (2, 5), (4, 7)]),
-    along_x([(0, 1), (2, 3)]),
-    along_x([(1, 2), (3, 0)]),
+HALVES = along_x([(0, 1), (2, 3)])
+STEPS = (
+    (
+        along_z([(0, 3), (1, 2), (4, 7), (5, 6)]),
+        along_z([(0, 2), (1, 3), (4, 6), (5, 7)]),
+        along_z([(0, 1), (2, 3), (4, 5), (6, 7)]),
+    ),
+    (along_z([(0, 7), (1, 6), (2, 5), (3, 4)]),),
 )
+BOTH = [
+    [(8 * x + z) * 8 + t for x in pair for t in range(8)] for pair in ((0, 1), (2, 3)) for z in range(8)
+]
 
 
 def local(momentum, grad):
     row_enc, col_enc, row_dec, col_dec = (jnp.asarray(t) for t in tables())
     momentum, grad = momentum[0], grad[0]
-    bands = encode(momentum, grad, row_enc, col_enc)
-    new_momentum = residual(momentum, grad, bands, row_dec, col_dec)
-    summed = bands
-    for step, pairs in enumerate(EXCHANGES):
-        summed = summed + lax.ppermute(summed, "dp", pairs)
-        if step == 2:
-            summed, new_momentum = lax.optimization_barrier((summed, new_momentum))
-    squares = jnp.sum((summed * summed).reshape(-1, 8, 128), axis=0)
-    energy = lax.all_to_all(jnp.broadcast_to(squares[None], (8, 8, 128)), "tensor", 0, 0)
-    update = decode(summed, energy.reshape(64, 128), row_dec, col_dec)
+    moment, bands, keep, send = encode(momentum, grad, row_enc, col_enc)
+    new_momentum = residual(moment, bands, row_dec, col_dec)
+    own = (
+        keep
+        + lax.ppermute(keep, "dp", along_x([(0, 2), (1, 3)]))
+        + lax.ppermute(send, "dp", along_x([(1, 2), (3, 0)]))
+        + lax.ppermute(send, "dp", HALVES)
+    )
+    for step in STEPS:
+        own = sum((lax.ppermute(own, "dp", pairs) for pairs in step), own)
+    other = lax.ppermute(own, "dp", HALVES)
+    squares = jnp.sum((own * own).reshape(-1, 8, 128), axis=0)
+    energy = lax.all_to_all(
+        jnp.broadcast_to(squares[None], (16, 8, 128)), ("dp", "tensor"), 0, 0, axis_index_groups=BOTH
+    )
+    update = decode(own, other, energy.reshape(128, 128), row_dec, col_dec)
     return (new_momentum[None], update)
 
 

time: 48.2 us -> 43.9 us (0.911)
  blocking collectives: 14.4 us -> 0 us
  starting transfers between devices: 14 us -> 22 us
  waiting for transfers between devices: 11.1 us -> 13.9 us
  Pallas kernels: 7.78 us -> 6.36 us
  local copies, waits for them, and re-layouts: 0.02 us -> 0.65 us
    all_to_all x1 -> x0, blocking collectives: 14.4 us -> none  [local(): lax.all_to_all(jnp.broadcast_to(squares[None], (8, 8, 128)), 'tensor', 0, 0)]
    all_to_all x0 -> x1, starting transfers between devices: none -> 8.97 us  [local(): lax.all_to_all(jnp.broadcast_to(squares[None], (16, 8, 128)), ('dp', 'ten...]
    all_to_all x0 -> x1, waiting for transfers between devices: none -> 1.57 us  [local(): lax.all_to_all(jnp.broadcast_to(squares[None], (16, 8, 128)), ('dp', 'ten...]
    pallas_call x1, Pallas kernels: 3.15 us -> 1.69 us  [residual(): pl.pallas_call(lambda *refs: residual_kernel(chunks, *refs), out_shape=ja...]
    ppermute x5 -> x8, waiting for transfers between devices: 11.1 us -> 12.3 us  [the longest x4 6.84 us: local(): own = sum((lax.ppermute(own, 'dp', pairs) for pairs in step), own)]
    ppermute x5 -> x8, starting transfers between devices: 14 us -> 13.1 us  [the longest x4 7.16 us: local(): own = sum((lax.ppermute(own, 'dp', pairs) for pairs in step), own)]
    broadcast_in_dim x1, local copies, waits for them, and re-layouts: 0.01 us -> 0.64 us  [local(): jnp.broadcast_to(squares[None], (16, 8, 128))]
  transfers between devices with their start and end apart: 5 -> 9, of which waited for: 5 -> 8; matrix products, arithmetic and copies ran while one was open for 0% -> 0% of each run, Pallas kernels for 7% -> 4%
where the time goes in v2:
time: 43.9 us; the launch traced here: 43.7 us
  starting transfers between devices  22 us (50%)
  waiting for transfers between devices  13.9 us (32%)
  Pallas kernels  6.36 us (14%)
  between operations  0.67 us (2%)
  local copies, waits for them, and re-layouts  0.65 us (1%)
    all_to_all x1, starting transfers between devices, local(): lax.all_to_all(jnp.broadcast_to(squares[None], (16, 8, 128)), ('dp', 'ten...  8.97 us
    ppermute x4, starting transfers between devices, local(): own = sum((lax.ppermute(own, 'dp', pairs) for pairs in step), own)  7.16 us
    ppermute x4, waiting for transfers between devices, local(): own = sum((lax.ppermute(own, 'dp', pairs) for pairs in step), own)  6.84 us
    ppermute x1, starting transfers between devices, local(): lax.ppermute(keep, 'dp', along_x([(0, 2), (1, 3)]))  3.66 us
    pallas_call x1, Pallas kernels, encode(): pl.pallas_call(lambda *refs: encode_kernel(chunks, *refs), out_shape=[jax...  2.88 us
    ppermute x1, waiting for transfers between devices, local(): lax.ppermute(send, 'dp', HALVES)  2.35 us
    pallas_call x1, Pallas kernels, decode(): pl.pallas_call(lambda *refs: update_kernel(chunks, *refs), out_shape=jax....  1.8 us
    pallas_call x1, Pallas kernels, residual(): pl.pallas_call(lambda *refs: residual_kernel(chunks, *refs), out_shape=ja...  1.69 us
  transfers between devices with their start and end apart: 9, of which 8 were waited for; matrix products, arithmetic and copies ran while one was open for 0% of the time, Pallas kernels for 4%

profile of v2, /device:TPU:1, one launch (start us, length us, event | category | flops | bytes accessed | tf_op | source)
XLA Modules:
  0.0 43.7 jit_solution(1072318559120480195)
XLA Ops:
  0.6 0.0 copy-start
  0.6 0.0 copy-start.1
  0.7 2.9 %encode.1 = (f32[7,128,512]{2,1,0:T(8,128)S(1)}, f32[224,128]{1,0:T(8,128)S(1)}, f32[112,128]{1,0:T(8,128)S(1)}, f32[112,128]{1,0:T(8,128)S(1)}) custom-call(f32[128,3584]{1,0:T(8,128)} %bitcast.7, bf16[128,3584]{1,0:T(8,128)(2,1)} %bitcast.9, bf16[64,256]{1,0:T(8,128)(2,1)} %constant.10.clone.refs_2_, bf16[512,256]{1,0:T(8,128)(2,1)} %constant.11.clone.refs_3_), custom_call_target="tpu_custom_call" | custom-call | flops 40000000 | bytes 3000000 | tf_op jit(solution)/shard_map/encode/pallas_call | solution.py:147
  3.5 3.7 %collective-permute-start = (f32[112,128]{1,0:T(8,128)S(1)}, f32[112,128]{1,0:T(8,128)S(1)}, u32[]{:S(2)}, u32[]{:S(2)}) collective-permute-start(f32[112,128]{1,0:T(8,128)S(1)} %get-tuple-element.8), channel_id=1, source_target_pairs={{0,128},{8,136},{16,144},{24,152},{32,160},{40,168},{48,176},{56,1... | collective-permute-start | bytes 172040 | tf_op jit(solution)/shard_map/ppermute | solution.py:241
  7.2 0.3 collective-permute-start.2
  7.5 0.6 %collective-permute-start.1 = (f32[112,128]{1,0:T(8,128)S(1)}, f32[112,128]{1,0:T(8,128)S(1)}, u32[]{:S(2)}, u32[]{:S(2)}) collective-permute-start(f32[112,128]{1,0:T(8,128)S(1)} %get-tuple-element.9), channel_id=1, source_target_pairs={{0,192},{8,200},{16,208},{24,216},{32,224},{40,232},{48,240},{56,2... | collective-permute-start | bytes 172040 | tf_op jit(solution)/shard_map/ppermute | solution.py:242
  8.1 0.7 %collective-permute-done = f32[112,128]{1,0:T(8,128)S(1)} collective-permute-done((f32[112,128]{1,0:T(8,128)S(1)}, f32[112,128]{1,0:T(8,128)S(1)}, u32[]{:S(2)}, u32[]{:S(2)}) %collective-permute-start) | collective-permute-done | bytes 57376 | tf_op jit(solution)/shard_map/ppermute | solution.py:241
  8.8 2.4 %collective-permute-done.2 = f32[112,128]{1,0:T(8,128)S(1)} collective-permute-done((f32[112,128]{1,0:T(8,128)S(1)}, f32[112,128]{1,0:T(8,128)S(1)}, u32[]{:S(2)}, u32[]{:S(2)}) %collective-permute-start.2) | collective-permute-done | bytes 57376 | tf_op jit(solution)/shard_map/ppermute | solution.py:243
  11.1 1.2 %collective-permute-done.1 = f32[112,128]{1,0:T(8,128)S(1)} collective-permute-done((f32[112,128]{1,0:T(8,128)S(1)}, f32[112,128]{1,0:T(8,128)S(1)}, u32[]{:S(2)}, u32[]{:S(2)}) %collective-permute-start.1) | collective-permute-done | bytes 57376 | tf_op jit(solution)/shard_map/ppermute | solution.py:242
  12.4 1.1 %collective-permute-start.5 = (f32[112,128]{1,0:T(8,128)S(1)}, f32[112,128]{1,0:T(8,128)S(1)}, u32[]{:S(2)}, u32[]{:S(2)}) collective-permute-start(f32[112,128]{1,0:T(8,128)S(1)} %add_add_fusion.1), channel_id=1, source_target_pairs={{0,8},{8,0},{16,24},{24,16},{32,40},{40,32},{48,56},{56,48},{64,72... | collective-permute-start | bytes 172040 | tf_op jit(solution)/shard_map/ppermute | solution.py:246
  13.5 3.0 %collective-permute-start.4 = (f32[112,128]{1,0:T(8,128)S(1)}, f32[112,128]{1,0:T(8,128)S(1)}, u32[]{:S(2)}, u32[]{:S(2)}) collective-permute-start(f32[112,128]{1,0:T(8,128)S(1)} %add_add_fusion.1), channel_id=1, source_target_pairs={{0,16},{8,24},{16,0},{24,8},{32,48},{40,56},{48,32},{56,40},{64,80... | collective-permute-start | bytes 172040 | tf_op jit(solution)/shard_map/ppermute | solution.py:246
  16.5 0.0 collective-permute-start.3
  16.5 0.0 collective-permute-done.5
  16.5 2.2 %collective-permute-done.4 = f32[112,128]{1,0:T(8,128)S(1)} collective-permute-done((f32[112,128]{1,0:T(8,128)S(1)}, f32[112,128]{1,0:T(8,128)S(1)}, u32[]{:S(2)}, u32[]{:S(2)}) %collective-permute-start.4) | collective-permute-done | bytes 57376 | tf_op jit(solution)/shard_map/ppermute | solution.py:246
  18.7 3.1 %collective-permute-done.3 = f32[112,128]{1,0:T(8,128)S(1)} collective-permute-done((f32[112,128]{1,0:T(8,128)S(1)}, f32[112,128]{1,0:T(8,128)S(1)}, u32[]{:S(2)}, u32[]{:S(2)}) %collective-permute-start.3) | collective-permute-done | bytes 57376 | tf_op jit(solution)/shard_map/ppermute | solution.py:246
  21.8 3.1 %collective-permute-start.6 = (f32[112,128]{1,0:T(8,128)S(1)}, f32[112,128]{1,0:T(8,128)S(1)}, u32[]{:S(2)}, u32[]{:S(2)}) collective-permute-start(f32[112,128]{1,0:T(8,128)S(1)} %add_add_fusion), channel_id=1, source_target_pairs={{0,56},{8,48},{16,40},{24,32},{32,24},{40,16},{48,8},{56,0},{64,12... | collective-permute-start | bytes 172040 | tf_op jit(solution)/shard_map/ppermute | solution.py:246
  24.8 1.6 %collective-permute-done.6 = f32[112,128]{1,0:T(8,128)S(1)} collective-permute-done((f32[112,128]{1,0:T(8,128)S(1)}, f32[112,128]{1,0:T(8,128)S(1)}, u32[]{:S(2)}, u32[]{:S(2)}) %collective-permute-start.6) | collective-permute-done | bytes 57376 | tf_op jit(solution)/shard_map/ppermute | solution.py:246
  26.4 0.6 %broadcast_in_dim.10 = f32[16,8,128]{2,1,0:T(8,128)} broadcast(f32[8,128]{1,0:T(8,128)S(1)} %get-tuple-element.10), dimensions={1,2} | broadcast | bytes 69632 | tf_op jit(solution)/shard_map/broadcast_in_dim | solution.py:250
  27.1 9.0 %all-to-all-start = ((f32[16,8,128]{2,1,0:T(8,128)}), f32[16,8,128]{2,1,0:T(8,128)S(1)}, u32[]{:S(2)}, u32[]{:S(2)}) async-start(f32[16,8,128]{2,1,0:T(8,128)} %broadcast_in_dim.10), calls=%async_computation | async-start | bytes 131072 | tf_op jit(solution)/shard_map/all_to_all | solution.py:249
  36.0 1.4 %collective-permute-start.7 = (f32[112,128]{1,0:T(8,128)S(1)}, f32[112,128]{1,0:T(8,128)S(1)}, u32[]{:S(2)}, u32[]{:S(2)}) collective-permute-start(f32[112,128]{1,0:T(8,128)S(1)} %get-tuple-element.11.refs_0_), channel_id=1, source_target_pairs={{0,64},{8,72},{16,80},{24,88},{32,96},{40,104},{48,112},{56,120},{... | collective-permute-start | bytes 172040 | tf_op jit(solution)/shard_map/ppermute | solution.py:247
  37.4 1.7 %residual.1 = f32[128,3584]{1,0:T(8,128)} custom-call(f32[7,128,512]{2,1,0:T(8,128)S(1)} %get-tuple-element.6.refs_0_, f32[224,128]{1,0:T(8,128)S(1)} %get-tuple-element.7.refs_1_, bf16[128,128]{1,0:T(8,128)(2,1)S(1)} %copy-done.1, bf16[384,512]{1,0:T(8,128)(2,1)S(1)} %copy-done), custom_call_target="tpu_custom_call" | custom-call | flops 40000000 | bytes 5000000 | tf_op jit(solution)/shard_map/residual/pallas_call | solution.py:169
  39.1 1.2 %collective-permute-done.7.refs_1_ = f32[112,128]{1,0:T(8,128)S(1)} collective-permute-done((f32[112,128]{1,0:T(8,128)S(1)}, f32[112,128]{1,0:T(8,128)S(1)}, u32[]{:S(2)}, u32[]{:S(2)}) %collective-permute-start.7) | collective-permute-done | bytes 57376 | tf_op jit(solution)/shard_map/ppermute | solution.py:247
  40.3 1.6 %all-to-all-done = f32[16,8,128]{2,1,0:T(8,128)S(1)} async-done(((f32[16,8,128]{2,1,0:T(8,128)}), f32[16,8,128]{2,1,0:T(8,128)S(1)}, u32[]{:S(2)}, u32[]{:S(2)}) %all-to-all-start) | async-done | bytes 65568 | tf_op jit(solution)/shard_map/all_to_all | solution.py:249
  41.9 1.8 %decode.1 = f32[128,3584]{1,0:T(8,128)} custom-call(f32[112,128]{1,0:T(8,128)S(1)} %get-tuple-element.11.refs_0_, f32[112,128]{1,0:T(8,128)S(1)} %collective-permute-done.7.refs_1_, f32[128,128]{1,0:T(8,128)S(1)} %bitcast.6, bf16[128,128]{1,0:T(8,128)(2,1)S(1)} %copy-done.1, bf16[384,512]{1,0:T(8,128)(2,1)S(1)} %copy-done), custom_call_target="tpu_custom_call" | custom-call | flops 40000000 | bytes 2000000 | tf_op jit(solution)/shard_map/decode/pallas_call | solution.py:187
  (5 shorter events, 0.1 us)
Async XLA Ops:
  0.6 36.8 %copy-start = (bf16[384,512]{1,0:T(8,128)(2,1)S(1)}, bf16[384,512]{1,0:T(8,128)(2,1)}, u32[]{:S(2)}) copy-start(bf16[384,512]{1,0:T(8,128)(2,1)} %constant.13.clone.refs_3_.refs_4_) | copy-start | bytes 1179652
  0.6 36.8 %copy-start.1 = (bf16[128,128]{1,0:T(8,128)(2,1)S(1)}, bf16[128,128]{1,0:T(8,128)(2,1)}, u32[]{:S(2)}) copy-start(bf16[128,128]{1,0:T(8,128)(2,1)} %constant.12.clone.refs_2_.refs_3_) | copy-start | bytes 98308
  3.5 5.2 %collective-permute-start = (f32[112,128]{1,0:T(8,128)S(1)}, f32[112,128]{1,0:T(8,128)S(1)}, u32[]{:S(2)}, u32[]{:S(2)}) collective-permute-start(f32[112,128]{1,0:T(8,128)S(1)} %get-tuple-element.8), channel_id=1, source_target_pairs={{0,128},{8,136},{16,144},{24,152},{32,160},{40,168},{48,176},{56,1... | collective-permute-start | bytes 172040 | tf_op jit(solution)/shard_map/ppermute | solution.py:241
  7.2 3.9 %collective-permute-start.2 = (f32[112,128]{1,0:T(8,128)S(1)}, f32[112,128]{1,0:T(8,128)S(1)}, u32[]{:S(2)}, u32[]{:S(2)}) collective-permute-start(f32[112,128]{1,0:T(8,128)S(1)} %get-tuple-element.9), channel_id=1, source_target_pairs={{0,64},{8,72},{16,80},{24,88},{32,96},{40,104},{48,112},{56,120},{... | collective-permute-start | bytes 172040 | tf_op jit(solution)/shard_map/ppermute | solution.py:243
  7.5 4.9 %collective-permute-start.1 = (f32[112,128]{1,0:T(8,128)S(1)}, f32[112,128]{1,0:T(8,128)S(1)}, u32[]{:S(2)}, u32[]{:S(2)}) collective-permute-start(f32[112,128]{1,0:T(8,128)S(1)} %get-tuple-element.9), channel_id=1, source_target_pairs={{0,192},{8,200},{16,208},{24,216},{32,224},{40,232},{48,240},{56,2... | collective-permute-start | bytes 172040 | tf_op jit(solution)/shard_map/ppermute | solution.py:242
  12.4 4.1 %collective-permute-start.5 = (f32[112,128]{1,0:T(8,128)S(1)}, f32[112,128]{1,0:T(8,128)S(1)}, u32[]{:S(2)}, u32[]{:S(2)}) collective-permute-start(f32[112,128]{1,0:T(8,128)S(1)} %add_add_fusion.1), channel_id=1, source_target_pairs={{0,8},{8,0},{16,24},{24,16},{32,40},{40,32},{48,56},{56,48},{64,72... | collective-permute-start | bytes 172040 | tf_op jit(solution)/shard_map/ppermute | solution.py:246
  13.5 5.2 %collective-permute-start.4 = (f32[112,128]{1,0:T(8,128)S(1)}, f32[112,128]{1,0:T(8,128)S(1)}, u32[]{:S(2)}, u32[]{:S(2)}) collective-permute-start(f32[112,128]{1,0:T(8,128)S(1)} %add_add_fusion.1), channel_id=1, source_target_pairs={{0,16},{8,24},{16,0},{24,8},{32,48},{40,56},{48,32},{56,40},{64,80... | collective-permute-start | bytes 172040 | tf_op jit(solution)/shard_map/ppermute | solution.py:246
  16.5 5.3 %collective-permute-start.3 = (f32[112,128]{1,0:T(8,128)S(1)}, f32[112,128]{1,0:T(8,128)S(1)}, u32[]{:S(2)}, u32[]{:S(2)}) collective-permute-start(f32[112,128]{1,0:T(8,128)S(1)} %add_add_fusion.1), channel_id=1, source_target_pairs={{0,24},{8,16},{16,8},{24,0},{32,56},{40,48},{48,40},{56,32},{64,88... | collective-permute-start | bytes 172040 | tf_op jit(solution)/shard_map/ppermute | solution.py:246
  21.8 4.6 %collective-permute-start.6 = (f32[112,128]{1,0:T(8,128)S(1)}, f32[112,128]{1,0:T(8,128)S(1)}, u32[]{:S(2)}, u32[]{:S(2)}) collective-permute-start(f32[112,128]{1,0:T(8,128)S(1)} %add_add_fusion), channel_id=1, source_target_pairs={{0,56},{8,48},{16,40},{24,32},{32,24},{40,16},{48,8},{56,0},{64,12... | collective-permute-start | bytes 172040 | tf_op jit(solution)/shard_map/ppermute | solution.py:246
  27.1 14.8 %all-to-all-start = ((f32[16,8,128]{2,1,0:T(8,128)}), f32[16,8,128]{2,1,0:T(8,128)S(1)}, u32[]{:S(2)}, u32[]{:S(2)}) async-start(f32[16,8,128]{2,1,0:T(8,128)} %broadcast_in_dim.10), calls=%async_computation | async-start | bytes 131072 | tf_op jit(solution)/shard_map/all_to_all | solution.py:249
  36.0 4.3 %collective-permute-start.7 = (f32[112,128]{1,0:T(8,128)S(1)}, f32[112,128]{1,0:T(8,128)S(1)}, u32[]{:S(2)}, u32[]{:S(2)}) collective-permute-start(f32[112,128]{1,0:T(8,128)S(1)} %get-tuple-element.11.refs_0_), channel_id=1, source_target_pairs={{0,64},{8,72},{16,80},{24,88},{32,96},{40,104},{48,112},{56,120},{... | collective-permute-start | bytes 172040 | tf_op jit(solution)/shard_map/ppermute | solution.py:247

commit v3 on v2

--- a/solution.py
+++ b/solution.py
@@ -81,13 +81,15 @@
         pair[1].start()
     tables_in[1].start()
     tables_in[0].wait()
-    for i in range(chunks):
-        copies[i][0].wait()
-        copies[i][1].wait()
-        moment = 0.999 * m[i] + g[i].astype(F32)
-        moment_ref[i] = moment
-        both = dot(row[...], jnp.concatenate(halves(moment), axis=0))
-        mixed[pl.ds(i * 32, 32), :] = both[:32] + both[32:]
+    for group in (range(1), range(1, chunks // 2 + 1), range(chunks // 2 + 1, chunks)):
+        for i in group:
+            copies[i][0].wait()
+            copies[i][1].wait()
+        for i in group:
+            moment = 0.999 * m[i] + g[i].astype(F32)
+            moment_ref[i] = moment
+            both = dot(row[...], jnp.concatenate(halves(moment), axis=0))
+            mixed[pl.ds(i * 32, 32), :] = both[:32] + both[32:]
     tables_in[1].wait()
     high, low = halves(mixed[...])
     first = dot(high, col[...])
@@ -97,19 +99,22 @@
     keep_ref[...], send_ref[...] = ordered(bands[:half], bands[half:])
 
 
-def expand(bands, row, col):
+def expand(bands, col):
     high, low = halves(bands)
     return dot(jnp.concatenate([high, low, high], axis=1), col)
 
 
+def stacked(part):
+    high, low = halves(part)
+    return jnp.concatenate([high, low, high, jnp.zeros_like(high)], axis=0)
+
+
 def rows_of(part, row):
-    high, low = halves(part)
-    stack = jnp.concatenate([high, low, high, jnp.zeros_like(high)], axis=0)
-    return dot(row, stack)
+    return dot(row, stacked(part))
 
 
 def residual_kernel(chunks, moment_ref, bands_ref, row_ref, col_ref, out_hbm, out, spread, sems):
-    spread[...] = expand(bands_ref[...], row_ref[...], col_ref[...])
+    spread[...] = expand(bands_ref[...], col_ref[...])
     stores = []
     for i in range(chunks):
         cols = pl.ds(i * CHUNK, CHUNK)
@@ -120,15 +125,20 @@
         store.wait()
 
 
-def update_kernel(chunks, own_ref, other_ref, energy_ref, row_ref, col_ref, out_hbm, out, spread, sems):
+def spread_kernel(chunks, own_ref, other_ref, col_ref, stack_ref):
+    bands = jnp.concatenate(ordered(own_ref[...], other_ref[...]), axis=0)
+    mixed = expand(bands, col_ref[...])
+    for i in range(chunks):
+        stack_ref[i] = stacked(mixed[i * 32 : (i + 1) * 32])
+
+
+def update_kernel(chunks, stack_ref, energy_ref, row_ref, out_hbm, out, sems):
     energy = jnp.sum(energy_ref[...])
-    scale = lax.rsqrt(jnp.full((1, 128), energy * (1.0 / (ROWS * FF)) + 1e-06, F32))
-    bands = jnp.concatenate(ordered(own_ref[...], other_ref[...]), axis=0)
-    spread[...] = expand(bands * scale, row_ref[...], col_ref[...])
+    scale = lax.rsqrt(jnp.full((1, CHUNK), energy * (1.0 / (ROWS * FF)) + 1e-06, F32))
     stores = []
     for i in range(chunks):
         cols = pl.ds(i * CHUNK, CHUNK)
-        out[i] = rows_of(spread[pl.ds(i * 32, 32), :], row_ref[...])
+        out[i] = dot(row_ref[...], stack_ref[i]) * scale
         stores.append(pltpu.make_async_copy(out.at[i], out_hbm.at[:, cols], sems.at[i]))
         stores[-1].start()
     for store in stores:
@@ -182,22 +192,34 @@
     )(moment, bands, row, col)
 
 
-def decode(own, other, energy, row, col):
+def spread(own, other, col):
     chunks = own.shape[0] // 16
+    return pl.pallas_call(
+        lambda *refs: spread_kernel(chunks, *refs),
+        out_shape=jax.ShapeDtypeStruct((chunks, 128, CHUNK), BF16),
+        in_specs=[VMEM] * 3,
+        out_specs=VMEM,
+        compiler_params=PARAMS,
+        cost_estimate=pl.CostEstimate(flops=4 * 10**7, bytes_accessed=10**6, transcendentals=0),
+        name="spread",
+    )(own, other, col)
+
+
+def decode(stack, energy, row):
+    chunks = stack.shape[0]
     return pl.pallas_call(
         lambda *refs: update_kernel(chunks, *refs),
         out_shape=jax.ShapeDtypeStruct((ROWS, chunks * CHUNK), F32),
-        in_specs=[VMEM] * 5,
+        in_specs=[VMEM] * 3,
         out_specs=HBM,
         scratch_shapes=[
             pltpu.VMEM((chunks, ROWS, CHUNK), F32),
-            pltpu.VMEM((chunks * 32, CHUNK), F32),
             pltpu.SemaphoreType.DMA((chunks,)),
         ],
         compiler_params=PARAMS,
         cost_estimate=pl.CostEstimate(flops=4 * 10**7, bytes_accessed=2 * 10**6, transcendentals=0),
         name="decode",
-    )(own, other, energy, row, col)
+    )(stack, energy, row)
 
 
 def partners(pairs):
@@ -244,12 +266,13 @@
     )
     for step in STEPS:
         own = sum((lax.ppermute(own, "dp", pairs) for pairs in step), own)
+    own, new_momentum = lax.optimization_barrier((own, new_momentum))
     other = lax.ppermute(own, "dp", HALVES)
     squares = jnp.sum((own * own).reshape(-1, 8, 128), axis=0)
     energy = lax.all_to_all(
         jnp.broadcast_to(squares[None], (16, 8, 128)), ("dp", "tensor"), 0, 0, axis_index_groups=BOTH
     )
-    update = decode(own, other, energy.reshape(128, 128), row_dec, col_dec)
+    update = decode(spread(own, other, col_dec), energy.reshape(128, 128), row_dec)
     return (new_momentum[None], update)
 
 

time: 43.9 us -> 43.2 us (0.984)
    ppermute x1, waiting for transfers between devices: 1.2 us -> 2.9 us  [local(): other = lax.ppermute(own, 'dp', HALVES)]
    ppermute x4, waiting for transfers between devices: 6.84 us -> 5.28 us  [local(): own = sum((lax.ppermute(own, 'dp', pairs) for pairs in step), own)]
  transfers between devices with their start and end apart: 9 -> 9, of which waited for: 8 -> 7; matrix products, arithmetic and copies ran while one was open for 0% -> 0% of each run, Pallas kernels for 4% -> 5%
where the time goes in v3:
time: 43.2 us; the launch traced here: 43.1 us
  starting transfers between devices  21.9 us (51%)
  waiting for transfers between devices  13.8 us (32%)
  Pallas kernels  6 us (14%)
  between operations  0.7 us (2%)
  local copies, waits for them, and re-layouts  0.65 us (2%)
    all_to_all x1, starting transfers between devices, local(): lax.all_to_all(jnp.broadcast_to(squares[None], (16, 8, 128)), ('dp', 'ten...  8.82 us
    ppermute x4, starting transfers between devices, local(): own = sum((lax.ppermute(own, 'dp', pairs) for pairs in step), own)  7.16 us
    ppermute x4, waiting for transfers between devices, local(): own = sum((lax.ppermute(own, 'dp', pairs) for pairs in step), own)  5.28 us
    ppermute x1, starting transfers between devices, local(): lax.ppermute(keep, 'dp', along_x([(0, 2), (1, 3)]))  3.66 us
    ppermute x1, waiting for transfers between devices, local(): other = lax.ppermute(own, 'dp', HALVES)  2.9 us
    pallas_call x1, Pallas kernels, encode(): pl.pallas_call(lambda *refs: encode_kernel(chunks, *refs), out_shape=[jax...  2.56 us
    ppermute x1, waiting for transfers between devices, local(): lax.ppermute(send, 'dp', HALVES)  2.35 us
    pallas_call x1, Pallas kernels, residual(): pl.pallas_call(lambda *refs: residual_kernel(chunks, *refs), out_shape=ja...  1.69 us
  transfers between devices with their start and end apart: 9, of which 7 were waited for; matrix products, arithmetic and copies ran while one was open for 0% of the time, Pallas kernels for 5%

profile of v3, /device:TPU:1, one launch (start us, length us, event | category | flops | bytes accessed | tf_op | source)
XLA Modules:
  0.0 43.1 jit_solution(3412400951175020921)
XLA Ops:
  0.6 0.0 copy-start
  0.6 0.0 copy-start.1
  0.7 2.6 %encode.1 = (f32[7,128,512]{2,1,0:T(8,128)S(1)}, f32[224,128]{1,0:T(8,128)S(1)}, f32[112,128]{1,0:T(8,128)S(1)}, f32[112,128]{1,0:T(8,128)S(1)}) custom-call(f32[128,3584]{1,0:T(8,128)} %bitcast.7, bf16[128,3584]{1,0:T(8,128)(2,1)} %bitcast.9, bf16[64,256]{1,0:T(8,128)(2,1)} %constant.10.clone.refs_2_, bf16[512,256]{1,0:T(8,128)(2,1)} %constant.11.clone.refs_3_), custom_call_target="tpu_custom_call" | custom-call | flops 40000000 | bytes 3000000 | tf_op jit(solution)/shard_map/encode/pallas_call | solution.py:157
  3.2 3.7 %collective-permute-start = (f32[112,128]{1,0:T(8,128)S(1)}, f32[112,128]{1,0:T(8,128)S(1)}, u32[]{:S(2)}, u32[]{:S(2)}) collective-permute-start(f32[112,128]{1,0:T(8,128)S(1)} %get-tuple-element.8), channel_id=1, source_target_pairs={{0,128},{8,136},{16,144},{24,152},{32,160},{40,168},{48,176},{56,1... | collective-permute-start | bytes 172040 | tf_op jit(solution)/shard_map/ppermute | solution.py:263
  6.9 0.3 collective-permute-start.2
  7.2 0.6 %collective-permute-start.1 = (f32[112,128]{1,0:T(8,128)S(1)}, f32[112,128]{1,0:T(8,128)S(1)}, u32[]{:S(2)}, u32[]{:S(2)}) collective-permute-start(f32[112,128]{1,0:T(8,128)S(1)} %get-tuple-element.9), channel_id=1, source_target_pairs={{0,192},{8,200},{16,208},{24,216},{32,224},{40,232},{48,240},{56,2... | collective-permute-start | bytes 172040 | tf_op jit(solution)/shard_map/ppermute | solution.py:264
  7.7 0.7 %collective-permute-done = f32[112,128]{1,0:T(8,128)S(1)} collective-permute-done((f32[112,128]{1,0:T(8,128)S(1)}, f32[112,128]{1,0:T(8,128)S(1)}, u32[]{:S(2)}, u32[]{:S(2)}) %collective-permute-start) | collective-permute-done | bytes 57376 | tf_op jit(solution)/shard_map/ppermute | solution.py:263
  8.4 2.4 %collective-permute-done.2 = f32[112,128]{1,0:T(8,128)S(1)} collective-permute-done((f32[112,128]{1,0:T(8,128)S(1)}, f32[112,128]{1,0:T(8,128)S(1)}, u32[]{:S(2)}, u32[]{:S(2)}) %collective-permute-start.2) | collective-permute-done | bytes 57376 | tf_op jit(solution)/shard_map/ppermute | solution.py:265
  10.8 1.2 %collective-permute-done.1 = f32[112,128]{1,0:T(8,128)S(1)} collective-permute-done((f32[112,128]{1,0:T(8,128)S(1)}, f32[112,128]{1,0:T(8,128)S(1)}, u32[]{:S(2)}, u32[]{:S(2)}) %collective-permute-start.1) | collective-permute-done | bytes 57376 | tf_op jit(solution)/shard_map/ppermute | solution.py:264
  12.1 1.1 %collective-permute-start.5 = (f32[112,128]{1,0:T(8,128)S(1)}, f32[112,128]{1,0:T(8,128)S(1)}, u32[]{:S(2)}, u32[]{:S(2)}) collective-permute-start(f32[112,128]{1,0:T(8,128)S(1)} %add_add_fusion.1), channel_id=1, source_target_pairs={{0,8},{8,0},{16,24},{24,16},{32,40},{40,32},{48,56},{56,48},{64,72... | collective-permute-start | bytes 172040 | tf_op jit(solution)/shard_map/ppermute | solution.py:268
  13.2 3.0 %collective-permute-start.4 = (f32[112,128]{1,0:T(8,128)S(1)}, f32[112,128]{1,0:T(8,128)S(1)}, u32[]{:S(2)}, u32[]{:S(2)}) collective-permute-start(f32[112,128]{1,0:T(8,128)S(1)} %add_add_fusion.1), channel_id=1, source_target_pairs={{0,16},{8,24},{16,0},{24,8},{32,48},{40,56},{48,32},{56,40},{64,80... | collective-permute-start | bytes 172040 | tf_op jit(solution)/shard_map/ppermute | solution.py:268
  16.2 0.0 collective-permute-done.5
  16.2 2.2 %collective-permute-done.4 = f32[112,128]{1,0:T(8,128)S(1)} collective-permute-done((f32[112,128]{1,0:T(8,128)S(1)}, f32[112,128]{1,0:T(8,128)S(1)}, u32[]{:S(2)}, u32[]{:S(2)}) %collective-permute-start.4) | collective-permute-done | bytes 57376 | tf_op jit(solution)/shard_map/ppermute | solution.py:268
  18.3 3.1 %collective-permute-done.3 = f32[112,128]{1,0:T(8,128)S(1)} collective-permute-done((f32[112,128]{1,0:T(8,128)S(1)}, f32[112,128]{1,0:T(8,128)S(1)}, u32[]{:S(2)}, u32[]{:S(2)}) %collective-permute-start.3) | collective-permute-done | bytes 57376 | tf_op jit(solution)/shard_map/ppermute | solution.py:268
  21.5 3.1 %collective-permute-start.6 = (f32[112,128]{1,0:T(8,128)S(1)}, f32[112,128]{1,0:T(8,128)S(1)}, u32[]{:S(2)}, u32[]{:S(2)}) collective-permute-start(f32[112,128]{1,0:T(8,128)S(1)} %add_add_fusion), channel_id=1, source_target_pairs={{0,56},{8,48},{16,40},{24,32},{32,24},{40,16},{48,8},{56,0},{64,12... | collective-permute-start | bytes 172040 | tf_op jit(solution)/shard_map/ppermute | solution.py:268
  24.5 1.7 %residual.1 = f32[128,3584]{1,0:T(8,128)} custom-call(f32[7,128,512]{2,1,0:T(8,128)S(1)} %get-tuple-element.10.refs_0_, f32[224,128]{1,0:T(8,128)S(1)} %get-tuple-element.11.refs_1_, bf16[128,128]{1,0:T(8,128)(2,1)S(1)} %copy-done.1, bf16[384,512]{1,0:T(8,128)(2,1)S(1)} %copy-done), custom_call_target="tpu_custom_call" | custom-call | flops 40000000 | bytes 5000000 | tf_op jit(solution)/shard_map/residual/pallas_call | solution.py:179
  26.2 0.0 collective-permute-done.6
  26.3 0.6 %broadcast_in_dim.10 = f32[16,8,128]{2,1,0:T(8,128)} broadcast(f32[8,128]{1,0:T(8,128)S(1)} %bitcast_reduce_fusion), dimensions={1,2} | broadcast | bytes 69632 | tf_op jit(solution)/shard_map/broadcast_in_dim | solution.py:273
  26.9 8.8 %all-to-all-start = ((f32[16,8,128]{2,1,0:T(8,128)}), f32[16,8,128]{2,1,0:T(8,128)S(1)}, u32[]{:S(2)}, u32[]{:S(2)}) async-start(f32[16,8,128]{2,1,0:T(8,128)} %broadcast_in_dim.10), calls=%async_computation | async-start | bytes 131072 | tf_op jit(solution)/shard_map/all_to_all | solution.py:272
  35.7 1.4 %collective-permute-start.7 = (f32[112,128]{1,0:T(8,128)S(1)}, f32[112,128]{1,0:T(8,128)S(1)}, u32[]{:S(2)}, u32[]{:S(2)}) collective-permute-start(f32[112,128]{1,0:T(8,128)S(1)} %add.27.refs_0_), channel_id=1, source_target_pairs={{0,64},{8,72},{16,80},{24,88},{32,96},{40,104},{48,112},{56,120},{... | collective-permute-start | bytes 172040 | tf_op jit(solution)/shard_map/ppermute | solution.py:270
  37.1 2.9 %collective-permute-done.7.refs_1_ = f32[112,128]{1,0:T(8,128)S(1)} collective-permute-done((f32[112,128]{1,0:T(8,128)S(1)}, f32[112,128]{1,0:T(8,128)S(1)}, u32[]{:S(2)}, u32[]{:S(2)}) %collective-permute-start.7) | collective-permute-done | bytes 57376 | tf_op jit(solution)/shard_map/ppermute | solution.py:270
  40.0 0.3 spread.1.refs_0_
  40.3 1.3 %all-to-all-done = f32[16,8,128]{2,1,0:T(8,128)S(1)} async-done(((f32[16,8,128]{2,1,0:T(8,128)}), f32[16,8,128]{2,1,0:T(8,128)S(1)}, u32[]{:S(2)}, u32[]{:S(2)}) %all-to-all-start) | async-done | bytes 65568 | tf_op jit(solution)/shard_map/all_to_all | solution.py:272
  41.6 1.5 %decode.1 = f32[128,3584]{1,0:T(8,128)} custom-call(bf16[7,128,512]{2,1,0:T(8,128)(2,1)S(1)} %spread.1.refs_0_, f32[128,128]{1,0:T(8,128)S(1)} %bitcast.6, bf16[128,128]{1,0:T(8,128)(2,1)S(1)} %copy-done.1), custom_call_target="tpu_custom_call" | custom-call | flops 40000000 | bytes 2000000 | tf_op jit(solution)/shard_map/decode/pallas_call | solution.py:210
  (7 shorter events, 0.1 us)
Async XLA Ops:
  0.6 23.9 %copy-start = (bf16[384,512]{1,0:T(8,128)(2,1)S(1)}, bf16[384,512]{1,0:T(8,128)(2,1)}, u32[]{:S(2)}) copy-start(bf16[384,512]{1,0:T(8,128)(2,1)} %constant.13.clone.refs_3_.refs_2_) | copy-start | bytes 1179652
  0.6 23.9 %copy-start.1 = (bf16[128,128]{1,0:T(8,128)(2,1)S(1)}, bf16[128,128]{1,0:T(8,128)(2,1)}, u32[]{:S(2)}) copy-start(bf16[128,128]{1,0:T(8,128)(2,1)} %constant.12.clone.refs_2_) | copy-start | bytes 98308
  3.2 5.2 %collective-permute-start = (f32[112,128]{1,0:T(8,128)S(1)}, f32[112,128]{1,0:T(8,128)S(1)}, u32[]{:S(2)}, u32[]{:S(2)}) collective-permute-start(f32[112,128]{1,0:T(8,128)S(1)} %get-tuple-element.8), channel_id=1, source_target_pairs={{0,128},{8,136},{16,144},{24,152},{32,160},{40,168},{48,176},{56,1... | collective-permute-start | bytes 172040 | tf_op jit(solution)/shard_map/ppermute | solution.py:263
  6.9 3.9 %collective-permute-start.2 = (f32[112,128]{1,0:T(8,128)S(1)}, f32[112,128]{1,0:T(8,128)S(1)}, u32[]{:S(2)}, u32[]{:S(2)}) collective-permute-start(f32[112,128]{1,0:T(8,128)S(1)} %get-tuple-element.9), channel_id=1, source_target_pairs={{0,64},{8,72},{16,80},{24,88},{32,96},{40,104},{48,112},{56,120},{... | collective-permute-start | bytes 172040 | tf_op jit(solution)/shard_map/ppermute | solution.py:265
  7.2 4.9 %collective-permute-start.1 = (f32[112,128]{1,0:T(8,128)S(1)}, f32[112,128]{1,0:T(8,128)S(1)}, u32[]{:S(2)}, u32[]{:S(2)}) collective-permute-start(f32[112,128]{1,0:T(8,128)S(1)} %get-tuple-element.9), channel_id=1, source_target_pairs={{0,192},{8,200},{16,208},{24,216},{32,224},{40,232},{48,240},{56,2... | collective-permute-start | bytes 172040 | tf_op jit(solution)/shard_map/ppermute | solution.py:264
  12.1 4.1 %collective-permute-start.5 = (f32[112,128]{1,0:T(8,128)S(1)}, f32[112,128]{1,0:T(8,128)S(1)}, u32[]{:S(2)}, u32[]{:S(2)}) collective-permute-start(f32[112,128]{1,0:T(8,128)S(1)} %add_add_fusion.1), channel_id=1, source_target_pairs={{0,8},{8,0},{16,24},{24,16},{32,40},{40,32},{48,56},{56,48},{64,72... | collective-permute-start | bytes 172040 | tf_op jit(solution)/shard_map/ppermute | solution.py:268
  13.2 5.2 %collective-permute-start.4 = (f32[112,128]{1,0:T(8,128)S(1)}, f32[112,128]{1,0:T(8,128)S(1)}, u32[]{:S(2)}, u32[]{:S(2)}) collective-permute-start(f32[112,128]{1,0:T(8,128)S(1)} %add_add_fusion.1), channel_id=1, source_target_pairs={{0,16},{8,24},{16,0},{24,8},{32,48},{40,56},{48,32},{56,40},{64,80... | collective-permute-start | bytes 172040 | tf_op jit(solution)/shard_map/ppermute | solution.py:268
  16.2 5.3 %collective-permute-start.3 = (f32[112,128]{1,0:T(8,128)S(1)}, f32[112,128]{1,0:T(8,128)S(1)}, u32[]{:S(2)}, u32[]{:S(2)}) collective-permute-start(f32[112,128]{1,0:T(8,128)S(1)} %add_add_fusion.1), channel_id=1, source_target_pairs={{0,24},{8,16},{16,8},{24,0},{32,56},{40,48},{48,40},{56,32},{64,88... | collective-permute-start | bytes 172040 | tf_op jit(solution)/shard_map/ppermute | solution.py:268
  21.5 4.8 %collective-permute-start.6 = (f32[112,128]{1,0:T(8,128)S(1)}, f32[112,128]{1,0:T(8,128)S(1)}, u32[]{:S(2)}, u32[]{:S(2)}) collective-permute-start(f32[112,128]{1,0:T(8,128)S(1)} %add_add_fusion), channel_id=1, source_target_pairs={{0,56},{8,48},{16,40},{24,32},{32,24},{40,16},{48,8},{56,0},{64,12... | collective-permute-start | bytes 172040 | tf_op jit(solution)/shard_map/ppermute | solution.py:268
  26.9 14.7 %all-to-all-start = ((f32[16,8,128]{2,1,0:T(8,128)}), f32[16,8,128]{2,1,0:T(8,128)S(1)}, u32[]{:S(2)}, u32[]{:S(2)}) async-start(f32[16,8,128]{2,1,0:T(8,128)} %broadcast_in_dim.10), calls=%async_computation | async-start | bytes 131072 | tf_op jit(solution)/shard_map/all_to_all | solution.py:272
  35.7 4.3 %collective-permute-start.7 = (f32[112,128]{1,0:T(8,128)S(1)}, f32[112,128]{1,0:T(8,128)S(1)}, u32[]{:S(2)}, u32[]{:S(2)}) collective-permute-start(f32[112,128]{1,0:T(8,128)S(1)} %add.27.refs_0_), channel_id=1, source_target_pairs={{0,64},{8,72},{16,80},{24,88},{32,96},{40,104},{48,112},{56,120},{... | collective-permute-start | bytes 172040 | tf_op jit(solution)/shard_map/ppermute | solution.py:270

commit v4 on v3

--- a/solution.py
+++ b/solution.py
@@ -242,9 +242,9 @@
 HALVES = along_x([(0, 1), (2, 3)])
 STEPS = (
     (
+        along_z([(0, 1), (2, 3), (4, 5), (6, 7)]),
+        along_z([(0, 2), (1, 3), (4, 6), (5, 7)]),
         along_z([(0, 3), (1, 2), (4, 7), (5, 6)]),
-        along_z([(0, 2), (1, 3), (4, 6), (5, 7)]),
-        along_z([(0, 1), (2, 3), (4, 5), (6, 7)]),
     ),
     (along_z([(0, 7), (1, 6), (2, 5), (3, 4)]),),
 )
@@ -260,9 +260,9 @@
     new_momentum = residual(moment, bands, row_dec, col_dec)
     own = (
         keep
+        + lax.ppermute(send, "dp", HALVES)
+        + lax.ppermute(send, "dp", along_x([(1, 2), (3, 0)]))
         + lax.ppermute(keep, "dp", along_x([(0, 2), (1, 3)]))
-        + lax.ppermute(send, "dp", along_x([(1, 2), (3, 0)]))
-        + lax.ppermute(send, "dp", HALVES)
     )
     for step in STEPS:
         own = sum((lax.ppermute(own, "dp", pairs) for pairs in step), own)

time: 43.2 us -> 41.8 us (0.968)
  waiting for transfers between devices: 13.8 us -> 12.4 us
    ppermute x1, waiting for transfers between devices: 2.35 us -> 0.01 us  [local(): lax.ppermute(send, 'dp', HALVES)]
    ppermute x1, waiting for transfers between devices: 1.25 us -> 3.39 us  [local(): lax.ppermute(send, 'dp', along_x([(1, 2), (3, 0)]))]
    ppermute x4, waiting for transfers between devices: 5.28 us -> 4.09 us  [local(): own = sum((lax.ppermute(own, 'dp', pairs) for pairs in step), own)]
  transfers between devices with their start and end apart: 9 -> 9, of which waited for: 7 -> 6; matrix products, arithmetic and copies ran while one was open for 0% -> 0% of each run, Pallas kernels for 5% -> 5%
where the time goes in v4:
time: 41.8 us; the launch traced here: 41.6 us
  starting transfers between devices  21.9 us (52%)
  waiting for transfers between devices  12.4 us (30%)
  Pallas kernels  5.99 us (14%)
  between operations  0.7 us (2%)
  local copies, waits for them, and re-layouts  0.65 us (2%)
    all_to_all x1, starting transfers between devices, local(): lax.all_to_all(jnp.broadcast_to(squares[None], (16, 8, 128)), ('dp', 'ten...  8.4 us
    ppermute x4, starting transfers between devices, local(): own = sum((lax.ppermute(own, 'dp', pairs) for pairs in step), own)  7.57 us
    ppermute x4, waiting for transfers between devices, local(): own = sum((lax.ppermute(own, 'dp', pairs) for pairs in step), own)  4.09 us
    ppermute x1, starting transfers between devices, local(): lax.ppermute(keep, 'dp', along_x([(0, 2), (1, 3)]))  3.66 us
    ppermute x1, waiting for transfers between devices, local(): lax.ppermute(send, 'dp', along_x([(1, 2), (3, 0)]))  3.39 us
    ppermute x1, waiting for transfers between devices, local(): other = lax.ppermute(own, 'dp', HALVES)  2.9 us
    pallas_call x1, Pallas kernels, encode(): pl.pallas_call(lambda *refs: encode_kernel(chunks, *refs), out_shape=[jax...  2.56 us
    pallas_call x1, Pallas kernels, residual(): pl.pallas_call(lambda *refs: residual_kernel(chunks, *refs), out_shape=ja...  1.68 us
  transfers between devices with their start and end apart: 9, of which 6 were waited for; matrix products, arithmetic and copies ran while one was open for 0% of the time, Pallas kernels for 5%

profile of v4, /device:TPU:1, one launch (start us, length us, event | category | flops | bytes accessed | tf_op | source)
XLA Modules:
  0.0 41.6 jit_solution(6170533979119968858)
XLA Ops:
  0.6 0.0 copy-start
  0.6 0.0 copy-start.1
  0.7 2.6 %encode.1 = (f32[7,128,512]{2,1,0:T(8,128)S(1)}, f32[224,128]{1,0:T(8,128)S(1)}, f32[112,128]{1,0:T(8,128)S(1)}, f32[112,128]{1,0:T(8,128)S(1)}) custom-call(f32[128,3584]{1,0:T(8,128)} %bitcast.7, bf16[128,3584]{1,0:T(8,128)(2,1)} %bitcast.9, bf16[64,256]{1,0:T(8,128)(2,1)} %constant.10.clone.refs_2_, bf16[512,256]{1,0:T(8,128)(2,1)} %constant.11.clone.refs_3_), custom_call_target="tpu_custom_call" | custom-call | flops 40000000 | bytes 3000000 | tf_op jit(solution)/shard_map/encode/pallas_call | solution.py:157
  3.2 3.7 %collective-permute-start.2 = (f32[112,128]{1,0:T(8,128)S(1)}, f32[112,128]{1,0:T(8,128)S(1)}, u32[]{:S(2)}, u32[]{:S(2)}) collective-permute-start(f32[112,128]{1,0:T(8,128)S(1)} %get-tuple-element.8), channel_id=1, source_target_pairs={{0,128},{8,136},{16,144},{24,152},{32,160},{40,168},{48,176},{56,1... | collective-permute-start | bytes 172040 | tf_op jit(solution)/shard_map/ppermute | solution.py:265
  6.9 0.9 %collective-permute-start.1 = (f32[112,128]{1,0:T(8,128)S(1)}, f32[112,128]{1,0:T(8,128)S(1)}, u32[]{:S(2)}, u32[]{:S(2)}) collective-permute-start(f32[112,128]{1,0:T(8,128)S(1)} %get-tuple-element.9), channel_id=1, source_target_pairs={{0,192},{8,200},{16,208},{24,216},{32,224},{40,232},{48,240},{56,2... | collective-permute-start | bytes 172040 | tf_op jit(solution)/shard_map/ppermute | solution.py:264
  7.7 0.0 collective-permute-start
  7.7 0.7 %collective-permute-done.2 = f32[112,128]{1,0:T(8,128)S(1)} collective-permute-done((f32[112,128]{1,0:T(8,128)S(1)}, f32[112,128]{1,0:T(8,128)S(1)}, u32[]{:S(2)}, u32[]{:S(2)}) %collective-permute-start.2) | collective-permute-done | bytes 57376 | tf_op jit(solution)/shard_map/ppermute | solution.py:265
  8.4 3.4 %collective-permute-done.1 = f32[112,128]{1,0:T(8,128)S(1)} collective-permute-done((f32[112,128]{1,0:T(8,128)S(1)}, f32[112,128]{1,0:T(8,128)S(1)}, u32[]{:S(2)}, u32[]{:S(2)}) %collective-permute-start.1) | collective-permute-done | bytes 57376 | tf_op jit(solution)/shard_map/ppermute | solution.py:264
  11.8 0.0 collective-permute-done
  11.9 3.7 %collective-permute-start.5 = (f32[112,128]{1,0:T(8,128)S(1)}, f32[112,128]{1,0:T(8,128)S(1)}, u32[]{:S(2)}, u32[]{:S(2)}) collective-permute-start(f32[112,128]{1,0:T(8,128)S(1)} %add_add_fusion.1), channel_id=1, source_target_pairs={{0,24},{8,16},{16,8},{24,0},{32,56},{40,48},{48,40},{56,32},{64,88... | collective-permute-start | bytes 172040 | tf_op jit(solution)/shard_map/ppermute | solution.py:268
  15.6 0.0 collective-permute-start.4
  15.6 0.4 collective-permute-start.3
  16.0 1.2 %collective-permute-done.5 = f32[112,128]{1,0:T(8,128)S(1)} collective-permute-done((f32[112,128]{1,0:T(8,128)S(1)}, f32[112,128]{1,0:T(8,128)S(1)}, u32[]{:S(2)}, u32[]{:S(2)}) %collective-permute-start.5) | collective-permute-done | bytes 57376 | tf_op jit(solution)/shard_map/ppermute | solution.py:268
  17.1 2.9 %collective-permute-done.4 = f32[112,128]{1,0:T(8,128)S(1)} collective-permute-done((f32[112,128]{1,0:T(8,128)S(1)}, f32[112,128]{1,0:T(8,128)S(1)}, u32[]{:S(2)}, u32[]{:S(2)}) %collective-permute-start.4) | collective-permute-done | bytes 57376 | tf_op jit(solution)/shard_map/ppermute | solution.py:268
  20.1 3.5 %collective-permute-start.6 = (f32[112,128]{1,0:T(8,128)S(1)}, f32[112,128]{1,0:T(8,128)S(1)}, u32[]{:S(2)}, u32[]{:S(2)}) collective-permute-start(f32[112,128]{1,0:T(8,128)S(1)} %add_add_fusion), channel_id=1, source_target_pairs={{0,56},{8,48},{16,40},{24,32},{32,24},{40,16},{48,8},{56,0},{64,12... | collective-permute-start | bytes 172040 | tf_op jit(solution)/shard_map/ppermute | solution.py:268
  23.5 1.7 %residual.1 = f32[128,3584]{1,0:T(8,128)} custom-call(f32[7,128,512]{2,1,0:T(8,128)S(1)} %get-tuple-element.10.refs_0_, f32[224,128]{1,0:T(8,128)S(1)} %get-tuple-element.11.refs_1_, bf16[128,128]{1,0:T(8,128)(2,1)S(1)} %copy-done.1, bf16[384,512]{1,0:T(8,128)(2,1)S(1)} %copy-done), custom_call_target="tpu_custom_call" | custom-call | flops 40000000 | bytes 5000000 | tf_op jit(solution)/shard_map/residual/pallas_call | solution.py:179
  25.2 0.0 collective-permute-done.6
  25.3 0.6 %broadcast_in_dim.10 = f32[16,8,128]{2,1,0:T(8,128)} broadcast(f32[8,128]{1,0:T(8,128)S(1)} %bitcast_reduce_fusion), dimensions={1,2} | broadcast | bytes 69632 | tf_op jit(solution)/shard_map/broadcast_in_dim | solution.py:273
  25.9 8.4 %all-to-all-start = ((f32[16,8,128]{2,1,0:T(8,128)}), f32[16,8,128]{2,1,0:T(8,128)S(1)}, u32[]{:S(2)}, u32[]{:S(2)}) async-start(f32[16,8,128]{2,1,0:T(8,128)} %broadcast_in_dim.10), calls=%async_computation | async-start | bytes 131072 | tf_op jit(solution)/shard_map/all_to_all | solution.py:272
  34.3 1.4 %collective-permute-start.7 = (f32[112,128]{1,0:T(8,128)S(1)}, f32[112,128]{1,0:T(8,128)S(1)}, u32[]{:S(2)}, u32[]{:S(2)}) collective-permute-start(f32[112,128]{1,0:T(8,128)S(1)} %add.27.refs_0_), channel_id=1, source_target_pairs={{0,64},{8,72},{16,80},{24,88},{32,96},{40,104},{48,112},{56,120},{... | collective-permute-start | bytes 172040 | tf_op jit(solution)/shard_map/ppermute | solution.py:270
  35.7 2.9 %collective-permute-done.7.refs_1_ = f32[112,128]{1,0:T(8,128)S(1)} collective-permute-done((f32[112,128]{1,0:T(8,128)S(1)}, f32[112,128]{1,0:T(8,128)S(1)}, u32[]{:S(2)}, u32[]{:S(2)}) %collective-permute-start.7) | collective-permute-done | bytes 57376 | tf_op jit(solution)/shard_map/ppermute | solution.py:270
  38.6 0.3 spread.1.refs_0_
  38.9 1.3 %all-to-all-done = f32[16,8,128]{2,1,0:T(8,128)S(1)} async-done(((f32[16,8,128]{2,1,0:T(8,128)}), f32[16,8,128]{2,1,0:T(8,128)S(1)}, u32[]{:S(2)}, u32[]{:S(2)}) %all-to-all-start) | async-done | bytes 65568 | tf_op jit(solution)/shard_map/all_to_all | solution.py:272
  40.2 1.5 %decode.1 = f32[128,3584]{1,0:T(8,128)} custom-call(bf16[7,128,512]{2,1,0:T(8,128)(2,1)S(1)} %spread.1.refs_0_, f32[128,128]{1,0:T(8,128)S(1)} %bitcast.6, bf16[128,128]{1,0:T(8,128)(2,1)S(1)} %copy-done.1), custom_call_target="tpu_custom_call" | custom-call | flops 40000000 | bytes 2000000 | tf_op jit(solution)/shard_map/decode/pallas_call | solution.py:210
  (7 shorter events, 0.1 us)
Async XLA Ops:
  0.6 22.9 %copy-start = (bf16[384,512]{1,0:T(8,128)(2,1)S(1)}, bf16[384,512]{1,0:T(8,128)(2,1)}, u32[]{:S(2)}) copy-start(bf16[384,512]{1,0:T(8,128)(2,1)} %constant.13.clone.refs_3_.refs_2_) | copy-start | bytes 1179652
  0.6 22.9 %copy-start.1 = (bf16[128,128]{1,0:T(8,128)(2,1)S(1)}, bf16[128,128]{1,0:T(8,128)(2,1)}, u32[]{:S(2)}) copy-start(bf16[128,128]{1,0:T(8,128)(2,1)} %constant.12.clone.refs_2_) | copy-start | bytes 98308
  3.2 5.2 %collective-permute-start.2 = (f32[112,128]{1,0:T(8,128)S(1)}, f32[112,128]{1,0:T(8,128)S(1)}, u32[]{:S(2)}, u32[]{:S(2)}) collective-permute-start(f32[112,128]{1,0:T(8,128)S(1)} %get-tuple-element.8), channel_id=1, source_target_pairs={{0,128},{8,136},{16,144},{24,152},{32,160},{40,168},{48,176},{56,1... | collective-permute-start | bytes 172040 | tf_op jit(solution)/shard_map/ppermute | solution.py:265
  6.9 5.0 %collective-permute-start.1 = (f32[112,128]{1,0:T(8,128)S(1)}, f32[112,128]{1,0:T(8,128)S(1)}, u32[]{:S(2)}, u32[]{:S(2)}) collective-permute-start(f32[112,128]{1,0:T(8,128)S(1)} %get-tuple-element.9), channel_id=1, source_target_pairs={{0,192},{8,200},{16,208},{24,216},{32,224},{40,232},{48,240},{56,2... | collective-permute-start | bytes 172040 | tf_op jit(solution)/shard_map/ppermute | solution.py:264
  7.7 4.1 %collective-permute-start = (f32[112,128]{1,0:T(8,128)S(1)}, f32[112,128]{1,0:T(8,128)S(1)}, u32[]{:S(2)}, u32[]{:S(2)}) collective-permute-start(f32[112,128]{1,0:T(8,128)S(1)} %get-tuple-element.9), channel_id=1, source_target_pairs={{0,64},{8,72},{16,80},{24,88},{32,96},{40,104},{48,112},{56,120},{... | collective-permute-start | bytes 172040 | tf_op jit(solution)/shard_map/ppermute | solution.py:263
  11.9 5.3 %collective-permute-start.5 = (f32[112,128]{1,0:T(8,128)S(1)}, f32[112,128]{1,0:T(8,128)S(1)}, u32[]{:S(2)}, u32[]{:S(2)}) collective-permute-start(f32[112,128]{1,0:T(8,128)S(1)} %add_add_fusion.1), channel_id=1, source_target_pairs={{0,24},{8,16},{16,8},{24,0},{32,56},{40,48},{48,40},{56,32},{64,88... | collective-permute-start | bytes 172040 | tf_op jit(solution)/shard_map/ppermute | solution.py:268
  15.6 4.5 %collective-permute-start.4 = (f32[112,128]{1,0:T(8,128)S(1)}, f32[112,128]{1,0:T(8,128)S(1)}, u32[]{:S(2)}, u32[]{:S(2)}) collective-permute-start(f32[112,128]{1,0:T(8,128)S(1)} %add_add_fusion.1), channel_id=1, source_target_pairs={{0,16},{8,24},{16,0},{24,8},{32,48},{40,56},{48,32},{56,40},{64,80... | collective-permute-start | bytes 172040 | tf_op jit(solution)/shard_map/ppermute | solution.py:268
  15.6 4.5 %collective-permute-start.3 = (f32[112,128]{1,0:T(8,128)S(1)}, f32[112,128]{1,0:T(8,128)S(1)}, u32[]{:S(2)}, u32[]{:S(2)}) collective-permute-start(f32[112,128]{1,0:T(8,128)S(1)} %add_add_fusion.1), channel_id=1, source_target_pairs={{0,8},{8,0},{16,24},{24,16},{32,40},{40,32},{48,56},{56,48},{64,72... | collective-permute-start | bytes 172040 | tf_op jit(solution)/shard_map/ppermute | solution.py:268
  20.1 5.2 %collective-permute-start.6 = (f32[112,128]{1,0:T(8,128)S(1)}, f32[112,128]{1,0:T(8,128)S(1)}, u32[]{:S(2)}, u32[]{:S(2)}) collective-permute-start(f32[112,128]{1,0:T(8,128)S(1)} %add_add_fusion), channel_id=1, source_target_pairs={{0,56},{8,48},{16,40},{24,32},{32,24},{40,16},{48,8},{56,0},{64,12... | collective-permute-start | bytes 172040 | tf_op jit(solution)/shard_map/ppermute | solution.py:268
  25.9 14.3 %all-to-all-start = ((f32[16,8,128]{2,1,0:T(8,128)}), f32[16,8,128]{2,1,0:T(8,128)S(1)}, u32[]{:S(2)}, u32[]{:S(2)}) async-start(f32[16,8,128]{2,1,0:T(8,128)} %broadcast_in_dim.10), calls=%async_computation | async-start | bytes 131072 | tf_op jit(solution)/shard_map/all_to_all | solution.py:272
  34.3 4.3 %collective-permute-start.7 = (f32[112,128]{1,0:T(8,128)S(1)}, f32[112,128]{1,0:T(8,128)S(1)}, u32[]{:S(2)}, u32[]{:S(2)}) collective-permute-start(f32[112,128]{1,0:T(8,128)S(1)} %add.27.refs_0_), channel_id=1, source_target_pairs={{0,64},{8,72},{16,80},{24,88},{32,96},{40,104},{48,112},{56,120},{... | collective-permute-start | bytes 172040 | tf_op jit(solution)/shard_map/ppermute | solution.py:270

commit v5 on v4

--- a/solution.py
+++ b/solution.py
@@ -266,7 +266,6 @@
     )
     for step in STEPS:
         own = sum((lax.ppermute(own, "dp", pairs) for pairs in step), own)
-    own, new_momentum = lax.optimization_barrier((own, new_momentum))
     other = lax.ppermute(own, "dp", HALVES)
     squares = jnp.sum((own * own).reshape(-1, 8, 128), axis=0)
     energy = lax.all_to_all(

time: 41.8 us -> 41.8 us (level)
    ppermute x1, waiting for transfers between devices: 2.9 us -> 1.2 us  [local(): other = lax.ppermute(own, 'dp', HALVES)]
    ppermute x4, waiting for transfers between devices: 4.09 us -> 5.75 us  [local(): own = sum((lax.ppermute(own, 'dp', pairs) for pairs in step), own)]
  transfers between devices with their start and end apart: 9 -> 9, of which waited for: 6 -> 7; matrix products, arithmetic and copies ran while one was open for 0% -> 0% of each run, Pallas kernels for 5% -> 5%
where the time goes in v5:
time: 41.8 us; the launch traced here: 41.6 us
  starting transfers between devices  21.9 us (52%)
  waiting for transfers between devices  12.3 us (29%)
  Pallas kernels  6 us (14%)
  between operations  0.69 us (2%)
  local copies, waits for them, and re-layouts  0.65 us (2%)
    all_to_all x1, starting transfers between devices, local(): lax.all_to_all(jnp.broadcast_to(squares[None], (16, 8, 128)), ('dp', 'ten...  8.44 us
    ppermute x4, starting transfers between devices, local(): own = sum((lax.ppermute(own, 'dp', pairs) for pairs in step), own)  7.57 us
    ppermute x4, waiting for transfers between devices, local(): own = sum((lax.ppermute(own, 'dp', pairs) for pairs in step), own)  5.75 us
    ppermute x1, starting transfers between devices, local(): lax.ppermute(keep, 'dp', along_x([(0, 2), (1, 3)]))  3.66 us
    ppermute x1, waiting for transfers between devices, local(): lax.ppermute(send, 'dp', along_x([(1, 2), (3, 0)]))  3.39 us
    pallas_call x1, Pallas kernels, encode(): pl.pallas_call(lambda *refs: encode_kernel(chunks, *refs), out_shape=[jax...  2.56 us
    pallas_call x1, Pallas kernels, residual(): pl.pallas_call(lambda *refs: residual_kernel(chunks, *refs), out_shape=ja...  1.68 us
    pallas_call x1, Pallas kernels, decode(): pl.pallas_call(lambda *refs: update_kernel(chunks, *refs), out_shape=jax....  1.47 us
  transfers between devices with their start and end apart: 9, of which 7 were waited for; matrix products, arithmetic and copies ran while one was open for 0% of the time, Pallas kernels for 5%

profile of v5, /device:TPU:1, one launch (start us, length us, event | category | flops | bytes accessed | tf_op | source)
XLA Modules:
  0.0 41.6 jit_solution(774562583251710313)
XLA Ops:
  0.6 0.0 copy-start
  0.6 0.0 copy-start.1
  0.7 2.6 %encode.1 = (f32[7,128,512]{2,1,0:T(8,128)S(1)}, f32[224,128]{1,0:T(8,128)S(1)}, f32[112,128]{1,0:T(8,128)S(1)}, f32[112,128]{1,0:T(8,128)S(1)}) custom-call(f32[128,3584]{1,0:T(8,128)} %bitcast.7, bf16[128,3584]{1,0:T(8,128)(2,1)} %bitcast.9, bf16[64,256]{1,0:T(8,128)(2,1)} %constant.10.clone.refs_2_, bf16[512,256]{1,0:T(8,128)(2,1)} %constant.11.clone.refs_3_), custom_call_target="tpu_custom_call" | custom-call | flops 40000000 | bytes 3000000 | tf_op jit(solution)/shard_map/encode/pallas_call | solution.py:157
  3.2 3.7 %collective-permute-start.2 = (f32[112,128]{1,0:T(8,128)S(1)}, f32[112,128]{1,0:T(8,128)S(1)}, u32[]{:S(2)}, u32[]{:S(2)}) collective-permute-start(f32[112,128]{1,0:T(8,128)S(1)} %get-tuple-element.8), channel_id=1, source_target_pairs={{0,128},{8,136},{16,144},{24,152},{32,160},{40,168},{48,176},{56,1... | collective-permute-start | bytes 172040 | tf_op jit(solution)/shard_map/ppermute | solution.py:265
  6.9 0.9 %collective-permute-start.1 = (f32[112,128]{1,0:T(8,128)S(1)}, f32[112,128]{1,0:T(8,128)S(1)}, u32[]{:S(2)}, u32[]{:S(2)}) collective-permute-start(f32[112,128]{1,0:T(8,128)S(1)} %get-tuple-element.9), channel_id=1, source_target_pairs={{0,192},{8,200},{16,208},{24,216},{32,224},{40,232},{48,240},{56,2... | collective-permute-start | bytes 172040 | tf_op jit(solution)/shard_map/ppermute | solution.py:264
  7.7 0.0 collective-permute-start
  7.7 0.7 %collective-permute-done.2 = f32[112,128]{1,0:T(8,128)S(1)} collective-permute-done((f32[112,128]{1,0:T(8,128)S(1)}, f32[112,128]{1,0:T(8,128)S(1)}, u32[]{:S(2)}, u32[]{:S(2)}) %collective-permute-start.2) | collective-permute-done | bytes 57376 | tf_op jit(solution)/shard_map/ppermute | solution.py:265
  8.4 3.4 %collective-permute-done.1 = f32[112,128]{1,0:T(8,128)S(1)} collective-permute-done((f32[112,128]{1,0:T(8,128)S(1)}, f32[112,128]{1,0:T(8,128)S(1)}, u32[]{:S(2)}, u32[]{:S(2)}) %collective-permute-start.1) | collective-permute-done | bytes 57376 | tf_op jit(solution)/shard_map/ppermute | solution.py:264
  11.8 0.0 collective-permute-done
  11.9 3.7 %collective-permute-start.5 = (f32[112,128]{1,0:T(8,128)S(1)}, f32[112,128]{1,0:T(8,128)S(1)}, u32[]{:S(2)}, u32[]{:S(2)}) collective-permute-start(f32[112,128]{1,0:T(8,128)S(1)} %add_add_fusion.1), channel_id=1, source_target_pairs={{0,24},{8,16},{16,8},{24,0},{32,56},{40,48},{48,40},{56,32},{64,88... | collective-permute-start | bytes 172040 | tf_op jit(solution)/shard_map/ppermute | solution.py:268
  15.6 0.0 collective-permute-start.4
  15.6 0.4 collective-permute-start.3
  16.0 1.2 %collective-permute-done.5 = f32[112,128]{1,0:T(8,128)S(1)} collective-permute-done((f32[112,128]{1,0:T(8,128)S(1)}, f32[112,128]{1,0:T(8,128)S(1)}, u32[]{:S(2)}, u32[]{:S(2)}) %collective-permute-start.5) | collective-permute-done | bytes 57376 | tf_op jit(solution)/shard_map/ppermute | solution.py:268
  17.1 2.9 %collective-permute-done.4 = f32[112,128]{1,0:T(8,128)S(1)} collective-permute-done((f32[112,128]{1,0:T(8,128)S(1)}, f32[112,128]{1,0:T(8,128)S(1)}, u32[]{:S(2)}, u32[]{:S(2)}) %collective-permute-start.4) | collective-permute-done | bytes 57376 | tf_op jit(solution)/shard_map/ppermute | solution.py:268
  20.1 3.5 %collective-permute-start.6 = (f32[112,128]{1,0:T(8,128)S(1)}, f32[112,128]{1,0:T(8,128)S(1)}, u32[]{:S(2)}, u32[]{:S(2)}) collective-permute-start(f32[112,128]{1,0:T(8,128)S(1)} %add_add_fusion), channel_id=1, source_target_pairs={{0,56},{8,48},{16,40},{24,32},{32,24},{40,16},{48,8},{56,0},{64,12... | collective-permute-start | bytes 172040 | tf_op jit(solution)/shard_map/ppermute | solution.py:268
  23.5 1.7 %collective-permute-done.6 = f32[112,128]{1,0:T(8,128)S(1)} collective-permute-done((f32[112,128]{1,0:T(8,128)S(1)}, f32[112,128]{1,0:T(8,128)S(1)}, u32[]{:S(2)}, u32[]{:S(2)}) %collective-permute-start.6) | collective-permute-done | bytes 57376 | tf_op jit(solution)/shard_map/ppermute | solution.py:268
  25.2 0.6 %broadcast_in_dim.10 = f32[16,8,128]{2,1,0:T(8,128)} broadcast(f32[8,128]{1,0:T(8,128)S(1)} %get-tuple-element.10), dimensions={1,2} | broadcast | bytes 69632 | tf_op jit(solution)/shard_map/broadcast_in_dim | solution.py:272
  25.9 8.4 %all-to-all-start = ((f32[16,8,128]{2,1,0:T(8,128)}), f32[16,8,128]{2,1,0:T(8,128)S(1)}, u32[]{:S(2)}, u32[]{:S(2)}) async-start(f32[16,8,128]{2,1,0:T(8,128)} %broadcast_in_dim.10), calls=%async_computation | async-start | bytes 131072 | tf_op jit(solution)/shard_map/all_to_all | solution.py:271
  34.3 1.4 %collective-permute-start.7 = (f32[112,128]{1,0:T(8,128)S(1)}, f32[112,128]{1,0:T(8,128)S(1)}, u32[]{:S(2)}, u32[]{:S(2)}) collective-permute-start(f32[112,128]{1,0:T(8,128)S(1)} %get-tuple-element.11.refs_0_), channel_id=1, source_target_pairs={{0,64},{8,72},{16,80},{24,88},{32,96},{40,104},{48,112},{56,120},{... | collective-permute-start | bytes 172040 | tf_op jit(solution)/shard_map/ppermute | solution.py:269
  35.7 1.7 %residual.1 = f32[128,3584]{1,0:T(8,128)} custom-call(f32[7,128,512]{2,1,0:T(8,128)S(1)} %get-tuple-element.6.refs_0_, f32[224,128]{1,0:T(8,128)S(1)} %get-tuple-element.7.refs_1_, bf16[128,128]{1,0:T(8,128)(2,1)S(1)} %copy-done.1, bf16[384,512]{1,0:T(8,128)(2,1)S(1)} %copy-done), custom_call_target="tpu_custom_call" | custom-call | flops 40000000 | bytes 5000000 | tf_op jit(solution)/shard_map/residual/pallas_call | solution.py:179
  37.4 1.2 %collective-permute-done.7.refs_1_ = f32[112,128]{1,0:T(8,128)S(1)} collective-permute-done((f32[112,128]{1,0:T(8,128)S(1)}, f32[112,128]{1,0:T(8,128)S(1)}, u32[]{:S(2)}, u32[]{:S(2)}) %collective-permute-start.7) | collective-permute-done | bytes 57376 | tf_op jit(solution)/shard_map/ppermute | solution.py:269
  38.6 0.3 spread.1.refs_0_
  38.9 1.3 %all-to-all-done = f32[16,8,128]{2,1,0:T(8,128)S(1)} async-done(((f32[16,8,128]{2,1,0:T(8,128)}), f32[16,8,128]{2,1,0:T(8,128)S(1)}, u32[]{:S(2)}, u32[]{:S(2)}) %all-to-all-start) | async-done | bytes 65568 | tf_op jit(solution)/shard_map/all_to_all | solution.py:271
  40.2 1.5 %decode.1 = f32[128,3584]{1,0:T(8,128)} custom-call(bf16[7,128,512]{2,1,0:T(8,128)(2,1)S(1)} %spread.1.refs_0_, f32[128,128]{1,0:T(8,128)S(1)} %bitcast.6, bf16[128,128]{1,0:T(8,128)(2,1)S(1)} %copy-done.1), custom_call_target="tpu_custom_call" | custom-call | flops 40000000 | bytes 2000000 | tf_op jit(solution)/shard_map/decode/pallas_call | solution.py:210
  (6 shorter events, 0.1 us)
Async XLA Ops:
  0.6 35.1 %copy-start = (bf16[384,512]{1,0:T(8,128)(2,1)S(1)}, bf16[384,512]{1,0:T(8,128)(2,1)}, u32[]{:S(2)}) copy-start(bf16[384,512]{1,0:T(8,128)(2,1)} %constant.13.clone.refs_3_.refs_2_) | copy-start | bytes 1179652
  0.6 35.1 %copy-start.1 = (bf16[128,128]{1,0:T(8,128)(2,1)S(1)}, bf16[128,128]{1,0:T(8,128)(2,1)}, u32[]{:S(2)}) copy-start(bf16[128,128]{1,0:T(8,128)(2,1)} %constant.12.clone.refs_2_) | copy-start | bytes 98308
  3.2 5.2 %collective-permute-start.2 = (f32[112,128]{1,0:T(8,128)S(1)}, f32[112,128]{1,0:T(8,128)S(1)}, u32[]{:S(2)}, u32[]{:S(2)}) collective-permute-start(f32[112,128]{1,0:T(8,128)S(1)} %get-tuple-element.8), channel_id=1, source_target_pairs={{0,128},{8,136},{16,144},{24,152},{32,160},{40,168},{48,176},{56,1... | collective-permute-start | bytes 172040 | tf_op jit(solution)/shard_map/ppermute | solution.py:265
  6.9 5.0 %collective-permute-start.1 = (f32[112,128]{1,0:T(8,128)S(1)}, f32[112,128]{1,0:T(8,128)S(1)}, u32[]{:S(2)}, u32[]{:S(2)}) collective-permute-start(f32[112,128]{1,0:T(8,128)S(1)} %get-tuple-element.9), channel_id=1, source_target_pairs={{0,192},{8,200},{16,208},{24,216},{32,224},{40,232},{48,240},{56,2... | collective-permute-start | bytes 172040 | tf_op jit(solution)/shard_map/ppermute | solution.py:264
  7.7 4.1 %collective-permute-start = (f32[112,128]{1,0:T(8,128)S(1)}, f32[112,128]{1,0:T(8,128)S(1)}, u32[]{:S(2)}, u32[]{:S(2)}) collective-permute-start(f32[112,128]{1,0:T(8,128)S(1)} %get-tuple-element.9), channel_id=1, source_target_pairs={{0,64},{8,72},{16,80},{24,88},{32,96},{40,104},{48,112},{56,120},{... | collective-permute-start | bytes 172040 | tf_op jit(solution)/shard_map/ppermute | solution.py:263
  11.9 5.3 %collective-permute-start.5 = (f32[112,128]{1,0:T(8,128)S(1)}, f32[112,128]{1,0:T(8,128)S(1)}, u32[]{:S(2)}, u32[]{:S(2)}) collective-permute-start(f32[112,128]{1,0:T(8,128)S(1)} %add_add_fusion.1), channel_id=1, source_target_pairs={{0,24},{8,16},{16,8},{24,0},{32,56},{40,48},{48,40},{56,32},{64,88... | collective-permute-start | bytes 172040 | tf_op jit(solution)/shard_map/ppermute | solution.py:268
  15.6 4.5 %collective-permute-start.4 = (f32[112,128]{1,0:T(8,128)S(1)}, f32[112,128]{1,0:T(8,128)S(1)}, u32[]{:S(2)}, u32[]{:S(2)}) collective-permute-start(f32[112,128]{1,0:T(8,128)S(1)} %add_add_fusion.1), channel_id=1, source_target_pairs={{0,16},{8,24},{16,0},{24,8},{32,48},{40,56},{48,32},{56,40},{64,80... | collective-permute-start | bytes 172040 | tf_op jit(solution)/shard_map/ppermute | solution.py:268
  15.6 4.5 %collective-permute-start.3 = (f32[112,128]{1,0:T(8,128)S(1)}, f32[112,128]{1,0:T(8,128)S(1)}, u32[]{:S(2)}, u32[]{:S(2)}) collective-permute-start(f32[112,128]{1,0:T(8,128)S(1)} %add_add_fusion.1), channel_id=1, source_target_pairs={{0,8},{8,0},{16,24},{24,16},{32,40},{40,32},{48,56},{56,48},{64,72... | collective-permute-start | bytes 172040 | tf_op jit(solution)/shard_map/ppermute | solution.py:268
  20.1 5.1 %collective-permute-start.6 = (f32[112,128]{1,0:T(8,128)S(1)}, f32[112,128]{1,0:T(8,128)S(1)}, u32[]{:S(2)}, u32[]{:S(2)}) collective-permute-start(f32[112,128]{1,0:T(8,128)S(1)} %add_add_fusion), channel_id=1, source_target_pairs={{0,56},{8,48},{16,40},{24,32},{32,24},{40,16},{48,8},{56,0},{64,12... | collective-permute-start | bytes 172040 | tf_op jit(solution)/shard_map/ppermute | solution.py:268
  25.9 14.3 %all-to-all-start = ((f32[16,8,128]{2,1,0:T(8,128)}), f32[16,8,128]{2,1,0:T(8,128)S(1)}, u32[]{:S(2)}, u32[]{:S(2)}) async-start(f32[16,8,128]{2,1,0:T(8,128)} %broadcast_in_dim.10), calls=%async_computation | async-start | bytes 131072 | tf_op jit(solution)/shard_map/all_to_all | solution.py:271
  34.3 4.3 %collective-permute-start.7 = (f32[112,128]{1,0:T(8,128)S(1)}, f32[112,128]{1,0:T(8,128)S(1)}, u32[]{:S(2)}, u32[]{:S(2)}) collective-permute-start(f32[112,128]{1,0:T(8,128)S(1)} %get-tuple-element.11.refs_0_), channel_id=1, source_target_pairs={{0,64},{8,72},{16,80},{24,88},{32,96},{40,104},{48,112},{56,120},{... | collective-permute-start | bytes 172040 | tf_op jit(solution)/shard_map/ppermute | solution.py:269

commit v6 on v5

--- a/solution.py
+++ b/solution.py
@@ -246,7 +246,7 @@
         along_z([(0, 2), (1, 3), (4, 6), (5, 7)]),
         along_z([(0, 3), (1, 2), (4, 7), (5, 6)]),
     ),
-    (along_z([(0, 7), (1, 6), (2, 5), (3, 4)]),),
+    (along_z([(0, 7), (1, 6), (2, 4), (3, 5)]),),
 )
 BOTH = [
     [(8 * x + z) * 8 + t for x in pair for t in range(8)] for pair in ((0, 1), (2, 3)) for z in range(8)

time: 41.8 us -> 41.8 us (level)
  no operation moved by 1% of the time
where the time goes in v6:
time: 41.8 us; the launch traced here: 41.6 us
  starting transfers between devices  21.9 us (52%)
  waiting for transfers between devices  12.3 us (29%)
  Pallas kernels  6 us (14%)
  between operations  0.69 us (2%)
  local copies, waits for them, and re-layouts  0.65 us (2%)
    all_to_all x1, starting transfers between devices, local(): lax.all_to_all(jnp.broadcast_to(squares[None], (16, 8, 128)), ('dp', 'ten...  8.44 us
    ppermute x4, starting transfers between devices, local(): own = sum((lax.ppermute(own, 'dp', pairs) for pairs in step), own)  7.57 us
    ppermute x4, waiting for transfers between devices, local(): own = sum((lax.ppermute(own, 'dp', pairs) for pairs in step), own)  5.75 us
    ppermute x1, starting transfers between devices, local(): lax.ppermute(keep, 'dp', along_x([(0, 2), (1, 3)]))  3.66 us
    ppermute x1, waiting for transfers between devices, local(): lax.ppermute(send, 'dp', along_x([(1, 2), (3, 0)]))  3.39 us
    pallas_call x1, Pallas kernels, encode(): pl.pallas_call(lambda *refs: encode_kernel(chunks, *refs), out_shape=[jax...  2.56 us
    pallas_call x1, Pallas kernels, residual(): pl.pallas_call(lambda *refs: residual_kernel(chunks, *refs), out_shape=ja...  1.68 us
    pallas_call x1, Pallas kernels, decode(): pl.pallas_call(lambda *refs: update_kernel(chunks, *refs), out_shape=jax....  1.47 us
  transfers between devices with their start and end apart: 9, of which 7 were waited for; matrix products, arithmetic and copies ran while one was open for 0% of the time, Pallas kernels for 5%

profile of v6, /device:TPU:1, one launch (start us, length us, event | category | flops | bytes accessed | tf_op | source)
XLA Modules:
  0.0 41.6 jit_solution(7819379763341769902)
XLA Ops:
  0.6 0.0 copy-start
  0.6 0.0 copy-start.1
  0.7 2.6 %encode.1 = (f32[7,128,512]{2,1,0:T(8,128)S(1)}, f32[224,128]{1,0:T(8,128)S(1)}, f32[112,128]{1,0:T(8,128)S(1)}, f32[112,128]{1,0:T(8,128)S(1)}) custom-call(f32[128,3584]{1,0:T(8,128)} %bitcast.7, bf16[128,3584]{1,0:T(8,128)(2,1)} %bitcast.9, bf16[64,256]{1,0:T(8,128)(2,1)} %constant.10.clone.refs_2_, bf16[512,256]{1,0:T(8,128)(2,1)} %constant.11.clone.refs_3_), custom_call_target="tpu_custom_call" | custom-call | flops 40000000 | bytes 3000000 | tf_op jit(solution)/shard_map/encode/pallas_call | solution.py:157
  3.2 3.7 %collective-permute-start.2 = (f32[112,128]{1,0:T(8,128)S(1)}, f32[112,128]{1,0:T(8,128)S(1)}, u32[]{:S(2)}, u32[]{:S(2)}) collective-permute-start(f32[112,128]{1,0:T(8,128)S(1)} %get-tuple-element.8), channel_id=1, source_target_pairs={{0,128},{8,136},{16,144},{24,152},{32,160},{40,168},{48,176},{56,1... | collective-permute-start | bytes 172040 | tf_op jit(solution)/shard_map/ppermute | solution.py:265
  6.9 0.9 %collective-permute-start.1 = (f32[112,128]{1,0:T(8,128)S(1)}, f32[112,128]{1,0:T(8,128)S(1)}, u32[]{:S(2)}, u32[]{:S(2)}) collective-permute-start(f32[112,128]{1,0:T(8,128)S(1)} %get-tuple-element.9), channel_id=1, source_target_pairs={{0,192},{8,200},{16,208},{24,216},{32,224},{40,232},{48,240},{56,2... | collective-permute-start | bytes 172040 | tf_op jit(solution)/shard_map/ppermute | solution.py:264
  7.7 0.0 collective-permute-start
  7.7 0.7 %collective-permute-done.2 = f32[112,128]{1,0:T(8,128)S(1)} collective-permute-done((f32[112,128]{1,0:T(8,128)S(1)}, f32[112,128]{1,0:T(8,128)S(1)}, u32[]{:S(2)}, u32[]{:S(2)}) %collective-permute-start.2) | collective-permute-done | bytes 57376 | tf_op jit(solution)/shard_map/ppermute | solution.py:265
  8.4 3.4 %collective-permute-done.1 = f32[112,128]{1,0:T(8,128)S(1)} collective-permute-done((f32[112,128]{1,0:T(8,128)S(1)}, f32[112,128]{1,0:T(8,128)S(1)}, u32[]{:S(2)}, u32[]{:S(2)}) %collective-permute-start.1) | collective-permute-done | bytes 57376 | tf_op jit(solution)/shard_map/ppermute | solution.py:264
  11.8 0.0 collective-permute-done
  11.9 3.7 %collective-permute-start.5 = (f32[112,128]{1,0:T(8,128)S(1)}, f32[112,128]{1,0:T(8,128)S(1)}, u32[]{:S(2)}, u32[]{:S(2)}) collective-permute-start(f32[112,128]{1,0:T(8,128)S(1)} %add_add_fusion.1), channel_id=1, source_target_pairs={{0,24},{8,16},{16,8},{24,0},{32,56},{40,48},{48,40},{56,32},{64,88... | collective-permute-start | bytes 172040 | tf_op jit(solution)/shard_map/ppermute | solution.py:268
  15.6 0.0 collective-permute-start.4
  15.6 0.4 collective-permute-start.3
  16.0 1.2 %collective-permute-done.5 = f32[112,128]{1,0:T(8,128)S(1)} collective-permute-done((f32[112,128]{1,0:T(8,128)S(1)}, f32[112,128]{1,0:T(8,128)S(1)}, u32[]{:S(2)}, u32[]{:S(2)}) %collective-permute-start.5) | collective-permute-done | bytes 57376 | tf_op jit(solution)/shard_map/ppermute | solution.py:268
  17.1 2.9 %collective-permute-done.4 = f32[112,128]{1,0:T(8,128)S(1)} collective-permute-done((f32[112,128]{1,0:T(8,128)S(1)}, f32[112,128]{1,0:T(8,128)S(1)}, u32[]{:S(2)}, u32[]{:S(2)}) %collective-permute-start.4) | collective-permute-done | bytes 57376 | tf_op jit(solution)/shard_map/ppermute | solution.py:268
  20.1 3.5 %collective-permute-start.6 = (f32[112,128]{1,0:T(8,128)S(1)}, f32[112,128]{1,0:T(8,128)S(1)}, u32[]{:S(2)}, u32[]{:S(2)}) collective-permute-start(f32[112,128]{1,0:T(8,128)S(1)} %add_add_fusion), channel_id=1, source_target_pairs={{0,56},{8,48},{16,32},{24,40},{32,16},{40,24},{48,8},{56,0},{64,12... | collective-permute-start | bytes 172040 | tf_op jit(solution)/shard_map/ppermute | solution.py:268
  23.5 1.7 %collective-permute-done.6 = f32[112,128]{1,0:T(8,128)S(1)} collective-permute-done((f32[112,128]{1,0:T(8,128)S(1)}, f32[112,128]{1,0:T(8,128)S(1)}, u32[]{:S(2)}, u32[]{:S(2)}) %collective-permute-start.6) | collective-permute-done | bytes 57376 | tf_op jit(solution)/shard_map/ppermute | solution.py:268
  25.2 0.6 %broadcast_in_dim.10 = f32[16,8,128]{2,1,0:T(8,128)} broadcast(f32[8,128]{1,0:T(8,128)S(1)} %get-tuple-element.10), dimensions={1,2} | broadcast | bytes 69632 | tf_op jit(solution)/shard_map/broadcast_in_dim | solution.py:272
  25.9 8.4 %all-to-all-start = ((f32[16,8,128]{2,1,0:T(8,128)}), f32[16,8,128]{2,1,0:T(8,128)S(1)}, u32[]{:S(2)}, u32[]{:S(2)}) async-start(f32[16,8,128]{2,1,0:T(8,128)} %broadcast_in_dim.10), calls=%async_computation | async-start | bytes 131072 | tf_op jit(solution)/shard_map/all_to_all | solution.py:271
  34.3 1.4 %collective-permute-start.7 = (f32[112,128]{1,0:T(8,128)S(1)}, f32[112,128]{1,0:T(8,128)S(1)}, u32[]{:S(2)}, u32[]{:S(2)}) collective-permute-start(f32[112,128]{1,0:T(8,128)S(1)} %get-tuple-element.11.refs_0_), channel_id=1, source_target_pairs={{0,64},{8,72},{16,80},{24,88},{32,96},{40,104},{48,112},{56,120},{... | collective-permute-start | bytes 172040 | tf_op jit(solution)/shard_map/ppermute | solution.py:269
  35.7 1.7 %residual.1 = f32[128,3584]{1,0:T(8,128)} custom-call(f32[7,128,512]{2,1,0:T(8,128)S(1)} %get-tuple-element.6.refs_0_, f32[224,128]{1,0:T(8,128)S(1)} %get-tuple-element.7.refs_1_, bf16[128,128]{1,0:T(8,128)(2,1)S(1)} %copy-done.1, bf16[384,512]{1,0:T(8,128)(2,1)S(1)} %copy-done), custom_call_target="tpu_custom_call" | custom-call | flops 40000000 | bytes 5000000 | tf_op jit(solution)/shard_map/residual/pallas_call | solution.py:179
  37.4 1.2 %collective-permute-done.7.refs_1_ = f32[112,128]{1,0:T(8,128)S(1)} collective-permute-done((f32[112,128]{1,0:T(8,128)S(1)}, f32[112,128]{1,0:T(8,128)S(1)}, u32[]{:S(2)}, u32[]{:S(2)}) %collective-permute-start.7) | collective-permute-done | bytes 57376 | tf_op jit(solution)/shard_map/ppermute | solution.py:269
  38.6 0.3 spread.1.refs_0_
  38.9 1.3 %all-to-all-done = f32[16,8,128]{2,1,0:T(8,128)S(1)} async-done(((f32[16,8,128]{2,1,0:T(8,128)}), f32[16,8,128]{2,1,0:T(8,128)S(1)}, u32[]{:S(2)}, u32[]{:S(2)}) %all-to-all-start) | async-done | bytes 65568 | tf_op jit(solution)/shard_map/all_to_all | solution.py:271
  40.2 1.5 %decode.1 = f32[128,3584]{1,0:T(8,128)} custom-call(bf16[7,128,512]{2,1,0:T(8,128)(2,1)S(1)} %spread.1.refs_0_, f32[128,128]{1,0:T(8,128)S(1)} %bitcast.6, bf16[128,128]{1,0:T(8,128)(2,1)S(1)} %copy-done.1), custom_call_target="tpu_custom_call" | custom-call | flops 40000000 | bytes 2000000 | tf_op jit(solution)/shard_map/decode/pallas_call | solution.py:210
  (6 shorter events, 0.1 us)
Async XLA Ops:
  0.6 35.1 %copy-start = (bf16[384,512]{1,0:T(8,128)(2,1)S(1)}, bf16[384,512]{1,0:T(8,128)(2,1)}, u32[]{:S(2)}) copy-start(bf16[384,512]{1,0:T(8,128)(2,1)} %constant.13.clone.refs_3_.refs_2_) | copy-start | bytes 1179652
  0.6 35.1 %copy-start.1 = (bf16[128,128]{1,0:T(8,128)(2,1)S(1)}, bf16[128,128]{1,0:T(8,128)(2,1)}, u32[]{:S(2)}) copy-start(bf16[128,128]{1,0:T(8,128)(2,1)} %constant.12.clone.refs_2_) | copy-start | bytes 98308
  3.2 5.2 %collective-permute-start.2 = (f32[112,128]{1,0:T(8,128)S(1)}, f32[112,128]{1,0:T(8,128)S(1)}, u32[]{:S(2)}, u32[]{:S(2)}) collective-permute-start(f32[112,128]{1,0:T(8,128)S(1)} %get-tuple-element.8), channel_id=1, source_target_pairs={{0,128},{8,136},{16,144},{24,152},{32,160},{40,168},{48,176},{56,1... | collective-permute-start | bytes 172040 | tf_op jit(solution)/shard_map/ppermute | solution.py:265
  6.9 5.0 %collective-permute-start.1 = (f32[112,128]{1,0:T(8,128)S(1)}, f32[112,128]{1,0:T(8,128)S(1)}, u32[]{:S(2)}, u32[]{:S(2)}) collective-permute-start(f32[112,128]{1,0:T(8,128)S(1)} %get-tuple-element.9), channel_id=1, source_target_pairs={{0,192},{8,200},{16,208},{24,216},{32,224},{40,232},{48,240},{56,2... | collective-permute-start | bytes 172040 | tf_op jit(solution)/shard_map/ppermute | solution.py:264
  7.7 4.1 %collective-permute-start = (f32[112,128]{1,0:T(8,128)S(1)}, f32[112,128]{1,0:T(8,128)S(1)}, u32[]{:S(2)}, u32[]{:S(2)}) collective-permute-start(f32[112,128]{1,0:T(8,128)S(1)} %get-tuple-element.9), channel_id=1, source_target_pairs={{0,64},{8,72},{16,80},{24,88},{32,96},{40,104},{48,112},{56,120},{... | collective-permute-start | bytes 172040 | tf_op jit(solution)/shard_map/ppermute | solution.py:263
  11.9 5.3 %collective-permute-start.5 = (f32[112,128]{1,0:T(8,128)S(1)}, f32[112,128]{1,0:T(8,128)S(1)}, u32[]{:S(2)}, u32[]{:S(2)}) collective-permute-start(f32[112,128]{1,0:T(8,128)S(1)} %add_add_fusion.1), channel_id=1, source_target_pairs={{0,24},{8,16},{16,8},{24,0},{32,56},{40,48},{48,40},{56,32},{64,88... | collective-permute-start | bytes 172040 | tf_op jit(solution)/shard_map/ppermute | solution.py:268
  15.6 4.5 %collective-permute-start.4 = (f32[112,128]{1,0:T(8,128)S(1)}, f32[112,128]{1,0:T(8,128)S(1)}, u32[]{:S(2)}, u32[]{:S(2)}) collective-permute-start(f32[112,128]{1,0:T(8,128)S(1)} %add_add_fusion.1), channel_id=1, source_target_pairs={{0,16},{8,24},{16,0},{24,8},{32,48},{40,56},{48,32},{56,40},{64,80... | collective-permute-start | bytes 172040 | tf_op jit(solution)/shard_map/ppermute | solution.py:268
  15.6 4.5 %collective-permute-start.3 = (f32[112,128]{1,0:T(8,128)S(1)}, f32[112,128]{1,0:T(8,128)S(1)}, u32[]{:S(2)}, u32[]{:S(2)}) collective-permute-start(f32[112,128]{1,0:T(8,128)S(1)} %add_add_fusion.1), channel_id=1, source_target_pairs={{0,8},{8,0},{16,24},{24,16},{32,40},{40,32},{48,56},{56,48},{64,72... | collective-permute-start | bytes 172040 | tf_op jit(solution)/shard_map/ppermute | solution.py:268
  20.1 5.1 %collective-permute-start.6 = (f32[112,128]{1,0:T(8,128)S(1)}, f32[112,128]{1,0:T(8,128)S(1)}, u32[]{:S(2)}, u32[]{:S(2)}) collective-permute-start(f32[112,128]{1,0:T(8,128)S(1)} %add_add_fusion), channel_id=1, source_target_pairs={{0,56},{8,48},{16,32},{24,40},{32,16},{40,24},{48,8},{56,0},{64,12... | collective-permute-start | bytes 172040 | tf_op jit(solution)/shard_map/ppermute | solution.py:268
  25.9 14.3 %all-to-all-start = ((f32[16,8,128]{2,1,0:T(8,128)}), f32[16,8,128]{2,1,0:T(8,128)S(1)}, u32[]{:S(2)}, u32[]{:S(2)}) async-start(f32[16,8,128]{2,1,0:T(8,128)} %broadcast_in_dim.10), calls=%async_computation | async-start | bytes 131072 | tf_op jit(solution)/shard_map/all_to_all | solution.py:271
  34.3 4.3 %collective-permute-start.7 = (f32[112,128]{1,0:T(8,128)S(1)}, f32[112,128]{1,0:T(8,128)S(1)}, u32[]{:S(2)}, u32[]{:S(2)}) collective-permute-start(f32[112,128]{1,0:T(8,128)S(1)} %get-tuple-element.11.refs_0_), channel_id=1, source_target_pairs={{0,64},{8,72},{16,80},{24,88},{32,96},{40,104},{48,112},{56,120},{... | collective-permute-start | bytes 172040 | tf_op jit(solution)/shard_map/ppermute | solution.py:269
